TPU v7x, 32 devices: a whole 2x2x4 slice. The times are simulated.
32 devices in a mesh: sec: 4 (over z), mpo: 8 (over y, x, core).
Axes of the slice: x: 2, y: 2, z: 4, core: 2. Of those that a mesh axis runs over, the one named last changes fastest.
Arguments:
- psi: bfloat16 [4, 512, 512], P('sec'), may hold values from -6 to 6
- left_env: bfloat16 [4, 32, 512, 512], P('sec', 'mpo'), may hold values from -0.046875 to 0.046875
- right_env: bfloat16 [4, 32, 512, 512], P('sec', 'mpo'), may hold values from -0.25 to 0.25
- dims: int32 [4, 2], P('sec'), may hold values from 1 to 16, as said below
- term_shift: int32 [32], P('mpo'), may hold values from -1 to 1, as said below
- connect: int32 [4, 32], P('sec', 'mpo'), may hold values 0 or 1
Outputs:
- h_psi: bfloat16 [4, 512, 512], P('sec', 'mpo')
Inputs may be any that keep to these rules, and one draw needn't show every extreme that they name: `dims`: some sector has both sizes equal to 16. `term_shift`: some term shifts by 1 and some by -1.
All inputs are finite; a program needn't handle non-finite values. No bound on the sum of `connect` on one device may be relied on, other than what follows from the above.
Results may differ from a plain program's by a relative error of at most 0.0049.
Values may be sent and summed in bfloat16 or wider, within the bound.
No kernel may reach another device: no remote copies, remote signals or barrier semaphores. Data moves between devices by JAX's collectives and lax.ppermute only.
A program may use at most 64 MiB of HBM per device.

v0:
```python
import jax
import jax.numpy as jnp
from jax import lax
from jax.sharding import PartitionSpec as P


def with_halo(cells, sides, width):
    for axis, dim in sides:
        count = lax.axis_size(axis)
        ends = count - 1
        head = lax.slice_in_dim(cells, 0, width, axis=dim)
        tail = lax.slice_in_dim(cells, cells.shape[dim] - width, cells.shape[dim], axis=dim)
        cells = jnp.concatenate(
            [
                lax.ppermute(tail, axis, [(i, (i + 1) % count) for i in range(ends)]),
                cells,
                lax.ppermute(head, axis, [((i + 1) % count, i) for i in range(ends)]),
            ],
            axis=dim,
        )
    return cells


def local(psi, left_env, right_env, dims, term_shift, connect):
    order = psi.shape[1]
    positions = jnp.arange(order)
    live = dims * 32
    keep = (positions[:, None] < live[0, 0]) & (positions[None, :] < live[0, 1])
    masked = psi * keep.astype(jnp.bfloat16)[None]
    beside_all = with_halo(masked, (("sec", 0),), 1)
    shifts = term_shift[:, None, None]
    sources = jnp.where(
        shifts == 1,
        beside_all[0][None],
        jnp.where(shifts == -1, beside_all[2][None], beside_all[1][None]),
    )
    sources = sources * connect[0].astype(jnp.bfloat16)[:, None, None]
    env_left = left_env[0]
    env_right = right_env[0]
    first = jnp.einsum("wij,wjk->wik", env_left, sources, preferred_element_type=jnp.float32)
    first = first.astype(jnp.bfloat16)
    partial_sum = jnp.einsum("wik,wkl->il", first, env_right, preferred_element_type=jnp.float32)
    partial_sum = partial_sum * keep.astype(jnp.float32)
    mine = lax.psum_scatter(partial_sum, "mpo", scatter_dimension=0, tiled=True)
    return mine.astype(jnp.bfloat16)[None]


def solution(mesh):
    placed = (
        P("sec", None, None),
        P("sec", "mpo", None, None),
        P("sec", "mpo", None, None),
        P("sec", None),
        P("mpo"),
        P("sec", "mpo"),
    )
    return jax.shard_map(
        local, mesh=mesh, in_specs=placed, out_specs=P("sec", "mpo", None), check_vma=False
    )
```

profile of v0, /device:TPU:0, one launch (start us, length us, event | category | flops | bytes accessed | tf_op | source)
XLA Modules:
  0.0 81.5 jit_solution(14211548952929276092)
XLA Ops:
  6.5 0.0 copy-start
  6.5 0.0 reduce-scatter.2.cloned.1.call-start
  6.5 0.8 broadcast_multiply_fusion
  7.3 0.6 fusion.41
  7.9 1.2 %iota_compare_fusion = (pred[512]{0:T(512)(128)(4,1)S(1)}, pred[512]{0:T(512)(128)(4,1)S(1)}) fusion(s32[]{:T(128)} %bitcast.1, s32[]{:T(128)} %bitcast), kind=kLoop, calls=%fused_computation.19 | loop fusion | flops 1024 | bytes 1032 | tf_op jit(solution)/shard_map/lt | solution.py:28
  9.1 1.3 %and_select_fusion = bf16[1,512,512]{2,1,0:T(8,128)(2,1)S(1)} fusion(bf16[1,512,512]{2,1,0:T(8,128)(2,1)} %param.6, pred[512]{0:T(512)(128)(4,1)S(1)} %get-tuple-element.9, pred[512]{0:T(512)(128)(4,1)S(1)} %get-tuple-element.10), kind=kLoop, calls=%fused_computation.17 | loop fusion | flops 524288 | bytes 1049600 | tf_op jit(solution)/shard_map/mul | solution.py:29
  10.4 1.3 %collective-permute-start.1 = (bf16[1,512,512]{2,1,0:T(8,128)(2,1)S(1)}, bf16[1,512,512]{2,1,0:T(8,128)(2,1)S(1)}, u32[]{:S(2)}, u32[]{:S(2)}) collective-permute-start(bf16[1,512,512]{2,1,0:T(8,128)(2,1)S(1)} %and_select_fusion), channel_id=1, source_target_pairs={{8,0},{16,8},{24,16},{9,1},{17,9},{25,17},{10,2},{18,10},{26,18},{... | collective-permute-start | bytes 1572872 | tf_op jit(solution)/shard_map/ppermute | solution.py:17
  11.7 5.6 %collective-permute-start = (bf16[1,512,512]{2,1,0:T(8,128)(2,1)S(1)}, bf16[1,512,512]{2,1,0:T(8,128)(2,1)S(1)}, u32[]{:S(2)}, u32[]{:S(2)}) collective-permute-start(bf16[1,512,512]{2,1,0:T(8,128)(2,1)S(1)} %and_select_fusion), channel_id=1, source_target_pairs={{0,8},{8,16},{16,24},{1,9},{9,17},{17,25},{2,10},{10,18},{18,26},{... | collective-permute-start | bytes 1572872 | tf_op jit(solution)/shard_map/ppermute | solution.py:15
  17.3 0.7 convert_bitcast_fusion.1
  18.0 0.7 broadcast_compare_fusion.1
  18.6 1.3 %fusion.42 = bf16[512,512]{1,0:T(8,128)(2,1)S(1)} fusion(bf16[1,512,512]{2,1,0:T(8,128)(2,1)} %param.6, pred[512]{0:T(512)(128)(4,1)S(1)} %get-tuple-element.9, pred[512]{0:T(512)(128)(4,1)S(1)} %get-tuple-element.10), kind=kLoop, calls=%fused_computation.26 | loop fusion | flops 524288 | bytes 1049600 | tf_op jit(solution)/shard_map/jit(_where)/broadcast_in_dim | solution.py:35
  19.9 7.4 %collective-permute-done.1 = bf16[1,512,512]{2,1,0:T(8,128)(2,1)S(1)} collective-permute-done((bf16[1,512,512]{2,1,0:T(8,128)(2,1)S(1)}, bf16[1,512,512]{2,1,0:T(8,128)(2,1)S(1)}, u32[]{:S(2)}, u32[]{:S(2)}) %collective-permute-start.1) | collective-permute-done | bytes 524320 | tf_op jit(solution)/shard_map/ppermute | solution.py:17
  27.3 1.2 %collective-permute-done = bf16[1,512,512]{2,1,0:T(8,128)(2,1)S(1)} collective-permute-done((bf16[1,512,512]{2,1,0:T(8,128)(2,1)S(1)}, bf16[1,512,512]{2,1,0:T(8,128)(2,1)S(1)}, u32[]{:S(2)}, u32[]{:S(2)}) %collective-permute-start) | collective-permute-done | bytes 524320 | tf_op jit(solution)/shard_map/ppermute | solution.py:15
  28.4 0.0 copy-start.1
  28.4 0.8 copy-done.1
  29.3 0.0 copy-done
  29.3 5.3 %fusion.24 = f32[512,512]{1,0:T(8,128)} fusion(bf16[1,4,512,512]{3,2,1,0:T(8,128)(2,1)S(1)} %copy-done, pred[4]{0:T(512)(128)(4,1)S(1)} %get-tuple-element.8, pred[4]{0:T(512)(128)(4,1)S(1)} %get-tuple-element.7, bf16[1,4,512,512]{3,2,1,0:T(8,128)(2,1)} %param.7, bf16[4]{0:T(256)(128)(2,1)S(1)} %convert_bitcast_fusion.1, bf16[512,512]{1,0:T(8,128)(2,1)S(1)} %fusion.42, ...), kind=kOutput, calls=%fused_computation.12 | convolution fusion | flops 2155347968 | bytes 6816784 | tf_op jit(solution)/shard_map/wik,wkl->il/dot_general | solution.py:42
  34.5 0.0 reduce-scatter.2.cloned.1.call-update
  34.6 38.5 %reduce-scatter.2.cloned.1.call-done = f32[64,512]{1,0:T(8,128)} async-done(((f32[512,512]{1,0:T(8,128)}), f32[64,512]{1,0:T(8,128)}) %reduce-scatter.2.cloned.1.call-update) | async-done | bytes 131088 | tf_op jit(solution)/shard_map/reduce_scatter | solution.py:44
  73.1 1.5 %convert_bitcast_fusion = bf16[1,64,512]{2,1,0:T(8,128)(2,1)} fusion(f32[64,512]{1,0:T(8,128)} %reduce-scatter.2.cloned.1.call-done), kind=kLoop, calls=%fused_computation.18 | loop fusion | flops 32768 | bytes 196608 | tf_op jit(solution)/shard_map/broadcast_in_dim | solution.py:45
Async XLA Ops:
  6.5 22.7 %copy-start = (bf16[1,4,512,512]{3,2,1,0:T(8,128)(2,1)S(1)}, bf16[1,4,512,512]{3,2,1,0:T(8,128)(2,1)}, u32[]{:S(2)}) copy-start(bf16[1,4,512,512]{3,2,1,0:T(8,128)(2,1)} %param.8) | copy-start | bytes 6291460
  6.5 66.5 %reduce-scatter.2.cloned.1.call-start = ((), (), s32[]{:S(2)}) async-start(), calls=%async_computation.1 | async-start | bytes 1179648 | tf_op jit(solution)/shard_map/reduce_scatter | solution.py:44
  10.4 16.8 %collective-permute-start.1 = (bf16[1,512,512]{2,1,0:T(8,128)(2,1)S(1)}, bf16[1,512,512]{2,1,0:T(8,128)(2,1)S(1)}, u32[]{:S(2)}, u32[]{:S(2)}) collective-permute-start(bf16[1,512,512]{2,1,0:T(8,128)(2,1)S(1)} %and_select_fusion), channel_id=1, source_target_pairs={{8,0},{16,8},{24,16},{9,1},{17,9},{25,17},{10,2},{18,10},{26,18},{... | collective-permute-start | bytes 1572872 | tf_op jit(solution)/shard_map/ppermute | solution.py:17
  11.7 16.7 %collective-permute-start = (bf16[1,512,512]{2,1,0:T(8,128)(2,1)S(1)}, bf16[1,512,512]{2,1,0:T(8,128)(2,1)S(1)}, u32[]{:S(2)}, u32[]{:S(2)}) collective-permute-start(bf16[1,512,512]{2,1,0:T(8,128)(2,1)S(1)} %and_select_fusion), channel_id=1, source_target_pairs={{0,8},{8,16},{16,24},{1,9},{9,17},{17,25},{2,10},{10,18},{18,26},{... | collective-permute-start | bytes 1572872 | tf_op jit(solution)/shard_map/ppermute | solution.py:15
  28.4 0.8 copy-start.1
Sparse Core Ops, SparseCore 0:
  34.7 38.3 reduce-scatter.1
where the time goes:
time: 81.8 us; the launch traced here: 81.5 us
  waiting for transfers between devices  47.1 us (58%)
  between operations  13.4 us (16%)
  other arithmetic  7.4 us (9%)
  starting transfers between devices  6.88 us (8%)
  matrix products  5.29 us (6%)
  local copies, waits for them, and re-layouts  1.39 us (2%)
    reduce_scatter x1, waiting for transfers between devices, local(): mine = lax.psum_scatter(partial_sum, 'mpo', scatter_dimension=0, tiled=True)  38.5 us
    ppermute x1, waiting for transfers between devices, with_halo(): lax.ppermute(head, axis, [((i + 1) % count, i) for i in range(ends)])  7.36 us
    ppermute x1, starting transfers between devices, with_halo(): lax.ppermute(tail, axis, [(i, (i + 1) % count) for i in range(ends)])  5.59 us
    dot_general x1, matrix products, local(): jnp.einsum('wik,wkl->il', first, env_right, preferred_element_type=jnp.fl...  5.29 us
  transfers between devices with their start and end apart: 3, of which 3 were waited for; matrix products, arithmetic and copies ran while one was open for 3% of the time, Pallas kernels for 0%

commit v1 on v0

v1 whole, which is shorter than its diff:
```python
import jax
import jax.numpy as jnp
from jax import lax
from jax.experimental import pallas as pl
from jax.experimental.pallas import tpu as pltpu
from jax.sharding import PartitionSpec as P

AXES = ("sec", "mpo")


def halo_pairs(sectors, group):
    def other(sector, place):
        upper = (sector + place) % 2 == 0
        return sector + 1 if upper else sector - 1

    pairs = []
    for sector in range(sectors):
        for place in range(group):
            there = other(sector, place)
            if 0 <= there < sectors:
                pairs.append((sector * group + place, there * group + place))
            elif group % 4 == 0:
                pairs.append((sector * group + place, sector * group + (place ^ 2)))
    return pairs


def bit_pairs(sectors, group, bit_of):
    pairs = []
    for sector in range(sectors):
        for place in range(group):
            partner = place ^ (1 << bit_of(place % 2))
            pairs.append((sector * group + place, sector * group + partner))
    return pairs


def compute_kernel(pick_ref, live_ref, sources_ref, left_ref, right_ref, out_ref, total):
    terms = left_ref.shape[0]
    total[...] = jnp.zeros_like(total)
    for term in range(terms):

        @pl.when(pick_ref[term] < 3)
        def _():
            source = sources_ref[pick_ref[term]]
            first = jnp.dot(left_ref[term], source, preferred_element_type=jnp.float32)
            total[...] += jnp.dot(
                first.astype(jnp.bfloat16), right_ref[term], preferred_element_type=jnp.float32
            )

    rows = lax.broadcasted_iota(jnp.int32, total.shape, 0)
    cols = lax.broadcasted_iota(jnp.int32, total.shape, 1)
    keep = (rows < live_ref[0]) & (cols < live_ref[1])
    out_ref[...] = jnp.where(keep, total[...], 0.0)


def compute(pick, live, sources, left, right):
    order = left.shape[1]
    whole = pl.BlockSpec(memory_space=pltpu.VMEM)
    scalar = pl.BlockSpec(memory_space=pltpu.SMEM)
    return pl.pallas_call(
        compute_kernel,
        in_specs=[scalar, scalar, whole, whole, whole],
        out_specs=whole,
        out_shape=jax.ShapeDtypeStruct((order, order), jnp.float32),
        scratch_shapes=[pltpu.VMEM((order, order), jnp.float32)],
        compiler_params=pltpu.CompilerParams(vmem_limit_bytes=32 * 1024 * 1024),
    )(pick, live, sources, left, right)


def local(psi, left_env, right_env, dims, term_shift, connect):
    sectors, group = lax.axis_size("sec"), lax.axis_size("mpo")
    sector, place = lax.axis_index("sec"), lax.axis_index("mpo")
    core = place % 2
    order = psi.shape[1]
    bits = group.bit_length() - 1

    positions = jnp.arange(order)
    live = dims[0] * 32
    keep = (positions[:, None] < live[0]) & (positions[None, :] < live[1])
    masked = psi[0] * keep.astype(jnp.bfloat16)

    got = lax.ppermute(masked, AXES, halo_pairs(sectors, group))
    swapped = lax.ppermute(got, AXES, bit_pairs(sectors, group, lambda c: 0))
    got_upper = (sector + place) % 2 == 0
    sources = jnp.stack([masked, got, swapped])
    where_below = jnp.where(got_upper, 2, 1)
    from_sector = sector - term_shift
    pick = jnp.where(term_shift == 0, 0, jnp.where(term_shift == 1, where_below, 3 - where_below))
    used = (connect[0] != 0) & (from_sector >= 0) & (from_sector < sectors)
    pick = jnp.where(used, pick, 3).astype(jnp.int32)

    total = compute(pick, live, sources, left_env[0], right_env[0])

    blocks = total.reshape((2,) * bits + (order // group, order))
    rest = list(range(1, bits))
    orders = [rest, rest[1:] + rest[:1]]

    def halves(value, side):
        kept = lax.dynamic_index_in_dim(value, side, 0, keepdims=False)
        sent = lax.dynamic_index_in_dim(value, 1 - side, 0, keepdims=False)
        return kept, sent.astype(jnp.bfloat16)

    kept, sent = halves(jnp.moveaxis(blocks, bits - 1, 0), core)
    came = lax.ppermute(sent, AXES, bit_pairs(sectors, group, lambda c: 0))
    summed = kept + came.astype(jnp.float32)
    arranged = [jnp.transpose(summed, [bits - 1 - b for b in o] + [bits - 1, bits]) for o in orders]
    summed = jnp.where(core == 0, arranged[0], arranged[1])
    for step_at in range(bits - 1):
        bit = jnp.where(core == 0, orders[0][step_at], orders[1][step_at])
        kept, sent = halves(summed, (place >> bit) & 1)
        came = lax.ppermute(
            sent, AXES, bit_pairs(sectors, group, lambda c, step_at=step_at: orders[c][step_at])
        )
        summed = kept + came.astype(jnp.float32)
    return summed.astype(jnp.bfloat16)[None]


def solution(mesh):
    placed = (
        P("sec", None, None),
        P("sec", "mpo", None, None),
        P("sec", "mpo", None, None),
        P("sec", None),
        P("mpo"),
        P("sec", "mpo"),
    )
    return jax.shard_map(
        local, mesh=mesh, in_specs=placed, out_specs=P("sec", "mpo", None), check_vma=False
    )
```

time: 81.8 us -> 33.2 us (0.41)
  waiting for transfers between devices: 47.1 us -> 13.5 us
  between operations: 13.4 us -> 0.1 us
  matrix products: 5.29 us -> 0 us
  starting transfers between devices: 6.88 us -> 9.9 us
  Pallas kernels: 0 us -> 1.44 us
  other arithmetic: 7.4 us -> 6.2 us
    reduce_scatter x1 -> x0, waiting for transfers between devices: 38.5 us -> none  [local(): mine = lax.psum_scatter(partial_sum, 'mpo', scatter_dimension=0, tiled=True)]
    dot_general x1 -> x0, matrix products: 5.29 us -> none  [local(): jnp.einsum('wik,wkl->il', first, env_right, preferred_element_type=jnp.fl...]
    ppermute x2 -> x5, waiting for transfers between devices: 8.54 us -> 13.5 us  [the longest x1 7.16 us: local(): got = lax.ppermute(masked, AXES, halo_pairs(sectors, group))]
    ppermute x2 -> x5, starting transfers between devices: 6.88 us -> 9.9 us  [the longest x2 4.82 us: local(): lax.ppermute(sent, AXES, bit_pairs(sectors, group, lambda c, step_at=step...]
    broadcast_in_dim x2 -> x1, other arithmetic: 2.8 us -> 0.64 us  [local(): return summed.astype(jnp.bfloat16)[None]]
    pallas_call x0 -> x1, Pallas kernels: none -> 1.44 us  [compute(): pl.pallas_call(compute_kernel, in_specs=[scalar, scalar, whole, whole, wh...]
    mul x2 -> x3, other arithmetic: 2.07 us -> 3.33 us  [the longest x2 2.67 us: local(): masked = psi[0] * keep.astype(jnp.bfloat16)]
  transfers between devices with their start and end apart: 3 -> 5, of which waited for: 3 -> 4; matrix products, arithmetic and copies ran while one was open for 3% -> 6% of each run, Pallas kernels for 0% -> 0%
where the time goes in v1:
time: 33.2 us; the launch traced here: 33.4 us
  waiting for transfers between devices  13.5 us (41%)
  starting transfers between devices  9.9 us (30%)
  other arithmetic  6.2 us (19%)
  local copies, waits for them, and re-layouts  2.2 us (7%)
  Pallas kernels  1.44 us (4%)
    ppermute x1, waiting for transfers between devices, local(): got = lax.ppermute(masked, AXES, halo_pairs(sectors, group))  7.16 us
    ppermute x2, waiting for transfers between devices, local(): lax.ppermute(sent, AXES, bit_pairs(sectors, group, lambda c, step_at=step...  5.19 us
    ppermute x2, starting transfers between devices, local(): lax.ppermute(sent, AXES, bit_pairs(sectors, group, lambda c, step_at=step...  4.82 us
    ppermute x1, starting transfers between devices, local(): got = lax.ppermute(masked, AXES, halo_pairs(sectors, group))  3.09 us
    mul x2, other arithmetic, local(): masked = psi[0] * keep.astype(jnp.bfloat16)  2.67 us
    ppermute x1, starting transfers between devices, local(): came = lax.ppermute(sent, AXES, bit_pairs(sectors, group, lambda c: 0))  1.99 us
    unnamed x4, local copies, waits for them, and re-layouts  1.48 us
    pallas_call x1, Pallas kernels, compute(): pl.pallas_call(compute_kernel, in_specs=[scalar, scalar, whole, whole, wh...  1.44 us
  transfers between devices with their start and end apart: 5, of which 4 were waited for; matrix products, arithmetic and copies ran while one was open for 6% of the time, Pallas kernels for 0%

profile of v1, /device:TPU:0, one launch (start us, length us, event | category | flops | bytes accessed | tf_op | source)
XLA Modules:
  0.0 33.4 jit_solution(13849160701453088725)
XLA Ops:
  0.0 0.7 %broadcast_multiply_fusion = (s32[1,2]{1,0:T(1,128)S(1)}, s32[2]{0:T(128)S(1)}) fusion(s32[1,2]{1,0:T(1,128)} %param.9), kind=kLoop, calls=%fused_computation.23 | loop fusion | flops 2 | bytes 24 | tf_op jit(solution)/shard_map/mul | solution.py:77
  0.7 0.6 %fusion.9 = (s32[1,1]{1,0:T(1,128)}, s32[1,1]{1,0:T(1,128)}) fusion(s32[1,2]{1,0:T(1,128)S(1)} %get-tuple-element.7), kind=kLoop, calls=%fused_computation.25 | loop fusion | bytes 16 | tf_op jit(solution)/shard_map/slice | solution.py:78
  1.3 1.3 %iota_compare_fusion = (pred[512]{0:T(512)(128)(4,1)S(1)}, pred[512]{0:T(512)(128)(4,1)S(1)}) fusion(s32[]{:T(128)} %bitcast.3, s32[]{:T(128)} %bitcast.2), kind=kLoop, calls=%fused_computation.16 | loop fusion | flops 1024 | bytes 1032 | tf_op jit(solution)/shard_map/lt | solution.py:78
  2.6 1.3 %and_select_fusion = bf16[512,512]{1,0:T(8,128)(2,1)S(1)} fusion(bf16[1,512,512]{2,1,0:T(8,128)(2,1)} %param.6, pred[512]{0:T(512)(128)(4,1)S(1)} %get-tuple-element.9, pred[512]{0:T(512)(128)(4,1)S(1)} %get-tuple-element.10), kind=kLoop, calls=%fused_computation.1 | loop fusion | flops 524288 | bytes 1049600 | tf_op jit(solution)/shard_map/mul | solution.py:79
  3.8 3.1 %collective-permute-start = (bf16[512,512]{1,0:T(8,128)(2,1)S(1)}, bf16[512,512]{1,0:T(8,128)(2,1)S(1)}, u32[]{:S(2)}, u32[]{:S(2)}) collective-permute-start(bf16[512,512]{1,0:T(8,128)(2,1)S(1)} %and_select_fusion), channel_id=1, source_target_pairs={{0,8},{1,3},{2,10},{3,1},{4,12},{5,7},{6,14},{7,5},{8,0},{9,17},{1... | collective-permute-start | bytes 1572872 | tf_op jit(solution)/shard_map/ppermute | solution.py:81
  6.9 7.2 %collective-permute-done = bf16[512,512]{1,0:T(8,128)(2,1)S(1)} collective-permute-done((bf16[512,512]{1,0:T(8,128)(2,1)S(1)}, bf16[512,512]{1,0:T(8,128)(2,1)S(1)}, u32[]{:S(2)}, u32[]{:S(2)}) %collective-permute-start) | collective-permute-done | bytes 524320 | tf_op jit(solution)/shard_map/ppermute | solution.py:81
  14.1 0.0 collective-permute-start.1
  14.1 0.7 %fusion.7.pick_ref = s32[4]{0:T(128)S(1)} fusion(s32[1,4]{1,0:T(1,128)} %param.11, s32[4]{0:T(128)} %param.10, s32[]{:T(128)S(6)} %sub.20, s32[]{:T(128)S(6)} %select_n.65, s32[]{:T(128)S(6)} %axis_index.25), kind=kLoop, calls=%fused_computation.20 | loop fusion | flops 44 | bytes 60 | tf_op jit(solution)/shard_map/jit(_where)/select_n | solution.py:89
  14.8 0.0 copy-start.1
  14.8 1.4 %and_select_fusion.1 = bf16[1,512,512]{2,1,0:T(8,128)(2,1)S(1)} fusion(bf16[1,512,512]{2,1,0:T(8,128)(2,1)} %param.6, pred[512]{0:T(512)(128)(4,1)S(1)} %get-tuple-element.9, pred[512]{0:T(512)(128)(4,1)S(1)} %get-tuple-element.10), kind=kLoop, calls=%fused_computation.2 | loop fusion | flops 524288 | bytes 1049600 | tf_op jit(solution)/shard_map/mul | solution.py:79
  16.2 0.0 collective-permute-done.1
  16.2 0.0 copy-start
  16.2 0.2 pad_maximum_fusion.sources_ref
  16.4 0.1 copy-done.1
  16.5 1.4 %copy-done = bf16[1,4,512,512]{3,2,1,0:T(8,128)(2,1)S(1)} copy-done((bf16[1,4,512,512]{3,2,1,0:T(8,128)(2,1)S(1)}, bf16[1,4,512,512]{3,2,1,0:T(8,128)(2,1)}, u32[]{:S(2)}) %copy-start) | copy-done | bytes 2097176
  17.9 1.4 %shard_map.64 = f32[512,512]{1,0:T(8,128)S(1)} custom-call(s32[4]{0:T(128)S(1)} %fusion.7.pick_ref, s32[2]{0:T(128)S(1)} %get-tuple-element.8.live_ref, bf16[3,512,512]{2,1,0:T(8,128)(2,1)S(1)} %pad_maximum_fusion.sources_ref, bf16[4,512,512]{2,1,0:T(8,128)(2,1)S(1)} %bitcast.49, bf16[4,512,512]{2,1,0:T(8,128)(2,1)S(1)} %bitcast.50), custom_call_target="tpu_custom_call" | custom-call | tf_op jit(solution)/shard_map/pallas_call | solution.py:59
  19.4 2.0 %collective-permute-start.2 = (bf16[2,2,64,512]{3,2,1,0:T(8,128)(2,1)S(1)}, bf16[2,2,64,512]{3,2,1,0:T(8,128)(2,1)S(1)}, u32[]{:S(2)}, u32[]{:S(2)}) collective-permute-start(bf16[2,2,64,512]{3,2,1,0:T(8,128)(2,1)S(1)} %fusion.1), channel_id=1, source_target_pairs={{0,1},{1,0},{2,3},{3,2},{4,5},{5,4},{6,7},{7,6},{8,9},{9,8},{10,11... | collective-permute-start | bytes 786440 | tf_op jit(solution)/shard_map/ppermute | solution.py:103
  21.4 1.2 %collective-permute-done.2 = bf16[2,2,64,512]{3,2,1,0:T(8,128)(2,1)S(1)} collective-permute-done((bf16[2,2,64,512]{3,2,1,0:T(8,128)(2,1)S(1)}, bf16[2,2,64,512]{3,2,1,0:T(8,128)(2,1)S(1)}, u32[]{:S(2)}, u32[]{:S(2)}) %collective-permute-start.2) | collective-permute-done | bytes 262176 | tf_op jit(solution)/shard_map/ppermute | solution.py:103
  22.5 0.1 copy_select_fusion
  22.6 2.7 %collective-permute-start.3 = (bf16[2,64,512]{2,1,0:T(8,128)(2,1)S(1)}, bf16[2,64,512]{2,1,0:T(8,128)(2,1)S(1)}, u32[]{:S(2)}, u32[]{:S(2)}) collective-permute-start(bf16[2,64,512]{2,1,0:T(8,128)(2,1)S(1)} %fusion.2), channel_id=1, source_target_pairs={{0,2},{1,5},{2,0},{3,7},{4,6},{5,1},{6,4},{7,3},{8,10},{9,13},{10,... | collective-permute-start | bytes 393224 | tf_op jit(solution)/shard_map/ppermute | solution.py:110
  25.4 2.9 %collective-permute-done.3 = bf16[2,64,512]{2,1,0:T(8,128)(2,1)S(1)} collective-permute-done((bf16[2,64,512]{2,1,0:T(8,128)(2,1)S(1)}, bf16[2,64,512]{2,1,0:T(8,128)(2,1)S(1)}, u32[]{:S(2)}, u32[]{:S(2)}) %collective-permute-start.3) | collective-permute-done | bytes 131104 | tf_op jit(solution)/shard_map/ppermute | solution.py:110
  28.4 2.1 %collective-permute-start.4 = (bf16[64,512]{1,0:T(8,128)(2,1)S(1)}, bf16[64,512]{1,0:T(8,128)(2,1)S(1)}, u32[]{:S(2)}, u32[]{:S(2)}) collective-permute-start(bf16[64,512]{1,0:T(8,128)(2,1)S(1)} %fusion.4), channel_id=1, source_target_pairs={{0,4},{1,3},{2,6},{3,1},{4,0},{5,7},{6,2},{7,5},{8,12},{9,11},{10,... | collective-permute-start | bytes 196616 | tf_op jit(solution)/shard_map/ppermute | solution.py:110
  30.5 2.2 %collective-permute-done.4 = bf16[64,512]{1,0:T(8,128)(2,1)S(1)} collective-permute-done((bf16[64,512]{1,0:T(8,128)(2,1)S(1)}, bf16[64,512]{1,0:T(8,128)(2,1)S(1)}, u32[]{:S(2)}, u32[]{:S(2)}) %collective-permute-start.4) | collective-permute-done | bytes 65568 | tf_op jit(solution)/shard_map/ppermute | solution.py:110
  32.7 0.6 %fusion.5 = bf16[1,64,512]{2,1,0:T(8,128)(2,1)} fusion(bf16[64,512]{1,0:T(8,128)(2,1)S(1)} %collective-permute-done.4, f32[2,64,512]{2,1,0:T(8,128)S(1)} %bitcast_add_fusion.1, s32[]{:T(128)S(6)} %select_n.76), kind=kLoop, calls=%fused_computation.15 | loop fusion | flops 98304 | bytes 262148 | tf_op jit(solution)/shard_map/broadcast_in_dim | solution.py:114
  (4 shorter events, 0.1 us)
Async XLA Ops:
  3.8 10.2 %collective-permute-start = (bf16[512,512]{1,0:T(8,128)(2,1)S(1)}, bf16[512,512]{1,0:T(8,128)(2,1)S(1)}, u32[]{:S(2)}, u32[]{:S(2)}) collective-permute-start(bf16[512,512]{1,0:T(8,128)(2,1)S(1)} %and_select_fusion), channel_id=1, source_target_pairs={{0,8},{1,3},{2,10},{3,1},{4,12},{5,7},{6,14},{7,5},{8,0},{9,17},{1... | collective-permute-start | bytes 1572872 | tf_op jit(solution)/shard_map/ppermute | solution.py:81
  14.1 2.1 %collective-permute-start.1 = (bf16[512,512]{1,0:T(8,128)(2,1)S(1)}, bf16[512,512]{1,0:T(8,128)(2,1)S(1)}, u32[]{:S(2)}, u32[]{:S(2)}) collective-permute-start(bf16[512,512]{1,0:T(8,128)(2,1)S(1)} %collective-permute-done), channel_id=1, source_target_pairs={{0,1},{1,0},{2,3},{3,2},{4,5},{5,4},{6,7},{7,6},{8,9},{9,8},{10,11... | collective-permute-start | bytes 1572872 | tf_op jit(solution)/shard_map/ppermute | solution.py:82
  14.8 1.7 %copy-start.1 = (bf16[1,4,512,512]{3,2,1,0:T(8,128)(2,1)S(1)}, bf16[1,4,512,512]{3,2,1,0:T(8,128)(2,1)}, u32[]{:S(2)}) copy-start(bf16[1,4,512,512]{3,2,1,0:T(8,128)(2,1)} %param.8) | copy-start | bytes 6291460
  16.2 1.7 %copy-start = (bf16[1,4,512,512]{3,2,1,0:T(8,128)(2,1)S(1)}, bf16[1,4,512,512]{3,2,1,0:T(8,128)(2,1)}, u32[]{:S(2)}) copy-start(bf16[1,4,512,512]{3,2,1,0:T(8,128)(2,1)} %param.7) | copy-start | bytes 6291460
  19.4 3.2 %collective-permute-start.2 = (bf16[2,2,64,512]{3,2,1,0:T(8,128)(2,1)S(1)}, bf16[2,2,64,512]{3,2,1,0:T(8,128)(2,1)S(1)}, u32[]{:S(2)}, u32[]{:S(2)}) collective-permute-start(bf16[2,2,64,512]{3,2,1,0:T(8,128)(2,1)S(1)} %fusion.1), channel_id=1, source_target_pairs={{0,1},{1,0},{2,3},{3,2},{4,5},{5,4},{6,7},{7,6},{8,9},{9,8},{10,11... | collective-permute-start | bytes 786440 | tf_op jit(solution)/shard_map/ppermute | solution.py:103
  22.6 5.7 %collective-permute-start.3 = (bf16[2,64,512]{2,1,0:T(8,128)(2,1)S(1)}, bf16[2,64,512]{2,1,0:T(8,128)(2,1)S(1)}, u32[]{:S(2)}, u32[]{:S(2)}) collective-permute-start(bf16[2,64,512]{2,1,0:T(8,128)(2,1)S(1)} %fusion.2), channel_id=1, source_target_pairs={{0,2},{1,5},{2,0},{3,7},{4,6},{5,1},{6,4},{7,3},{8,10},{9,13},{10,... | collective-permute-start | bytes 393224 | tf_op jit(solution)/shard_map/ppermute | solution.py:110
  28.4 4.4 %collective-permute-start.4 = (bf16[64,512]{1,0:T(8,128)(2,1)S(1)}, bf16[64,512]{1,0:T(8,128)(2,1)S(1)}, u32[]{:S(2)}, u32[]{:S(2)}) collective-permute-start(bf16[64,512]{1,0:T(8,128)(2,1)S(1)} %fusion.4), channel_id=1, source_target_pairs={{0,4},{1,3},{2,6},{3,1},{4,0},{5,7},{6,2},{7,5},{8,12},{9,11},{10,... | collective-permute-start | bytes 196616 | tf_op jit(solution)/shard_map/ppermute | solution.py:110

commit v2 on v0

v2 whole, which is shorter than its diff:
```python
import functools

import jax
import jax.numpy as jnp
from jax import lax
from jax.experimental import pallas as pl
from jax.experimental.pallas import tpu as pltpu
from jax.sharding import PartitionSpec as P

AXES = ("sec", "mpo")
CUTS = (256, 256)
VMEM = pl.BlockSpec(memory_space=pltpu.VMEM)
HBM = pl.BlockSpec(memory_space=pltpu.HBM)
PARAMS = pltpu.CompilerParams(vmem_limit_bytes=8 * 1024 * 1024)


def halo_pairs(sectors, group):
    pairs = []
    for sector in range(sectors):
        for place in range(group):
            there = sector + 1 if (sector + place) % 2 == 0 else sector - 1
            if 0 <= there < sectors:
                pairs.append((sector * group + place, there * group + place))
            elif group % 4 == 0:
                pairs.append((sector * group + place, sector * group + (place ^ 2)))
    return pairs


def group_pairs(sectors, group, flip_of):
    return [
        (sector * group + place, sector * group + (place ^ flip_of(place % 2)))
        for sector in range(sectors)
        for place in range(group)
    ]


def in_hbm(array):
    return pltpu.with_memory_space_constraint(array, pltpu.HBM)


def dot(a, b):
    return jnp.dot(a, b, preferred_element_type=jnp.float32)


def mask_kernel(dims_hbm, psi_hbm, *refs):
    *out_refs, dims_ref, psi_ref, sems = refs
    copies = [
        pltpu.make_async_copy(dims_hbm, dims_ref, sems.at[0]),
        pltpu.make_async_copy(psi_hbm.at[0], psi_ref, sems.at[1]),
    ]
    for copy in copies:
        copy.start()
    for copy in copies:
        copy.wait()
    start = 0
    for out_ref in out_refs:
        shape = out_ref.shape
        rows = lax.broadcasted_iota(jnp.int32, shape, 0)
        cols = lax.broadcasted_iota(jnp.int32, shape, 1) + start
        keep = (rows < dims_ref[0, 0] * 32) & (cols < dims_ref[0, 1] * 32)
        piece = psi_ref[:, start : start + shape[1]]
        out_ref[...] = jnp.where(keep, piece, jnp.zeros_like(piece))
        start += shape[1]


def mask(dims, psi):
    order = psi.shape[1]
    return pl.pallas_call(
        mask_kernel,
        in_specs=[HBM, HBM],
        out_specs=[VMEM] * len(CUTS),
        out_shape=[jax.ShapeDtypeStruct((order, cut), jnp.bfloat16) for cut in CUTS],
        scratch_shapes=[
            pltpu.SMEM(dims.shape, jnp.int32),
            pltpu.VMEM(psi.shape[1:], psi.dtype),
            pltpu.SemaphoreType.DMA((2,)),
        ],
        compiler_params=PARAMS,
    )(in_hbm(dims), in_hbm(psi))


def own_kernel(sectors, shift_hbm, connect_hbm, *refs):
    *pieces, left_hbm, right_hbm, total_ref, left_ref, right_ref, code_ref, shift_ref, connect_ref, sems = refs
    terms = left_ref.shape[0]
    scalars = [
        pltpu.make_async_copy(shift_hbm, shift_ref, sems.at[2 * terms]),
        pltpu.make_async_copy(connect_hbm, connect_ref, sems.at[2 * terms + 1]),
    ]
    loads = []
    for copy in scalars:
        copy.start()
    for term in range(terms):
        pair = [
            pltpu.make_async_copy(left_hbm.at[0, term], left_ref.at[term], sems.at[2 * term]),
            pltpu.make_async_copy(right_hbm.at[0, term], right_ref.at[term], sems.at[2 * term + 1]),
        ]
        for copy in pair:
            copy.start()
        loads.append(pair)
    total_ref[...] = jnp.zeros_like(total_ref)
    for copy in scalars:
        copy.wait()

    sector, place = lax.axis_index("sec"), lax.axis_index("mpo")
    above = (sector + place) % 2 == 0
    code = jnp.int32(0)
    for term in range(terms):
        shift = shift_ref[term]
        there = sector - shift
        used = (shift != 0) & (connect_ref[0, term] != 0) & (there >= 0) & (there < sectors)
        direct = (shift < 0) == above
        code += jnp.where(used, jnp.where(direct, 2, 1), 0) << (2 * term)
    code_ref[...] = jnp.full(code_ref.shape, code, jnp.int32)

    for term in range(terms):
        for copy in loads[term]:
            copy.wait()

    @pl.loop(0, terms)
    def _(term):
        @pl.when((shift_ref[term] == 0) & (connect_ref[0, term] != 0))
        def _():
            start = 0
            for piece in pieces:
                first = dot(left_ref[term], piece[...]).astype(jnp.bfloat16)
                total_ref[...] += dot(first, right_ref[term, pl.ds(start, piece.shape[1])])
                start += piece.shape[1]


def own(sectors, term_shift, connect, pieces, left, right):
    _, terms, order, _ = left.shape
    return pl.pallas_call(
        functools.partial(own_kernel, sectors),
        in_specs=[HBM, HBM] + [VMEM] * len(pieces) + [HBM, HBM],
        out_specs=[VMEM] * 4,
        out_shape=[
            jax.ShapeDtypeStruct((order, order), jnp.float32),
            jax.ShapeDtypeStruct(left.shape[1:], left.dtype),
            jax.ShapeDtypeStruct(right.shape[1:], right.dtype),
            jax.ShapeDtypeStruct((8, 128), jnp.int32),
        ],
        scratch_shapes=[
            pltpu.SMEM(term_shift.shape, jnp.int32),
            pltpu.SMEM(connect.shape, jnp.int32),
            pltpu.SemaphoreType.DMA((2 * terms + 2,)),
        ],
        compiler_params=PARAMS,
        cost_estimate=pl.CostEstimate(flops=4 * terms * order**3, bytes_accessed=4 * terms * order**2, transcendentals=0),
    )(in_hbm(term_shift), in_hbm(connect), *pieces, in_hbm(left), in_hbm(right))


def add_terms(start, code_ref, sources, left_ref, right_ref, total_ref):
    code = code_ref[0, 0]

    @pl.loop(0, left_ref.shape[0])
    def _(term):
        choice = (code >> (2 * term)) & 3
        for which, source_ref in sources:

            @pl.when(choice == which)
            def _():
                width = source_ref.shape[1]
                first = dot(left_ref[term], source_ref[...]).astype(jnp.bfloat16)
                total_ref[...] += dot(first, right_ref[term, pl.ds(start, width)])


def shifted_kernel(start, code_ref, got_ref, swapped_ref, left_ref, right_ref, before_ref, total_ref):
    total_ref[...] = before_ref[...]
    add_terms(start, code_ref, ((2, got_ref), (1, swapped_ref)), left_ref, right_ref, total_ref)


def shifted(start, code, got, swapped, left, right, total):
    return pl.pallas_call(
        functools.partial(shifted_kernel, start),
        in_specs=[VMEM] * 6,
        out_specs=VMEM,
        out_shape=jax.ShapeDtypeStruct(total.shape, total.dtype),
        compiler_params=PARAMS,
    )(code, got, swapped, left, right, total)


def last_kernel(start, dims_hbm, code_ref, got_ref, swapped_ref, left_ref, right_ref, before_ref, kept_ref, sent_ref, total_ref, dims_ref, sem):
    copy = pltpu.make_async_copy(dims_hbm, dims_ref, sem)
    copy.start()
    total_ref[...] = before_ref[...]
    add_terms(start, code_ref, ((2, got_ref), (1, swapped_ref)), left_ref, right_ref, total_ref)
    copy.wait()
    order = total_ref.shape[0]
    blocks, height, _ = kept_ref.shape
    core = lax.axis_index("mpo") % 2
    for out_ref, side in ((sent_ref, 1 - core), (kept_ref, core)):
        for block in range(blocks):
            first = pl.multiple_of((2 * block + side) * height, height)
            rows = lax.broadcasted_iota(jnp.int32, (height, order), 0) + first
            cols = lax.broadcasted_iota(jnp.int32, (height, order), 1)
            keep = (rows < dims_ref[0, 0] * 32) & (cols < dims_ref[0, 1] * 32)
            out_ref[block] = jnp.where(keep, total_ref[pl.ds(first, height), :], 0.0).astype(out_ref.dtype)


def last(start, group, dims, code, got, swapped, left, right, total):
    order = total.shape[0]
    half = (group // 2, order // group, order)
    return pl.pallas_call(
        functools.partial(last_kernel, start),
        in_specs=[HBM] + [VMEM] * 6,
        out_specs=[VMEM, VMEM],
        out_shape=[jax.ShapeDtypeStruct(half, jnp.float32), jax.ShapeDtypeStruct(half, jnp.bfloat16)],
        scratch_shapes=[
            pltpu.VMEM((order, order), jnp.float32),
            pltpu.SMEM(dims.shape, jnp.int32),
            pltpu.SemaphoreType.DMA,
        ],
        compiler_params=PARAMS,
    )(in_hbm(dims), code, got, swapped, left, right, total)


def local(psi, left_env, right_env, dims, term_shift, connect):
    sectors, group = lax.axis_size("sec"), lax.axis_size("mpo")
    place = lax.axis_index("mpo")

    pieces = mask(dims, psi)
    to_core = group_pairs(sectors, group, lambda core: 1)
    got = [lax.ppermute(piece, AXES, halo_pairs(sectors, group)) for piece in pieces]
    total, left, right, code = own(sectors, term_shift, connect, pieces, left_env, right_env)
    got[0], total = lax.optimization_barrier((got[0], total))
    swapped = [lax.ppermute(piece, AXES, to_core) for piece in got]
    start = 0
    for at in range(len(CUTS) - 1):
        total = shifted(start, code, got[at], swapped[at], left, right, total)
        start += CUTS[at]
    kept, sent = last(start, group, dims, code, got[-1], swapped[-1], left, right, total)

    came = lax.ppermute(sent, AXES, to_core)
    value = kept + came.astype(jnp.float32)
    bits = (group // 2).bit_length() - 1
    while bits:
        taken = min(bits, 2)
        bits -= taken
        value = value.reshape((1 << taken, 1 << bits) + value.shape[1:])
        digit = (place >> (1 + bits)) & ((1 << taken) - 1)
        flips = [(1, 2, 3), (2, 1, 3)] if taken == 2 else [(1,), (1,)]
        arrived = []
        for even, odd in zip(*flips):
            flip = jnp.where(place % 2 == 0, even, odd)
            sent = lax.dynamic_index_in_dim(value, digit ^ flip, 0, keepdims=False).astype(jnp.bfloat16)
            partners = group_pairs(sectors, group, lambda core: (odd if core else even) << (1 + bits))
            arrived.append(lax.ppermute(sent, AXES, partners))
        value = lax.dynamic_index_in_dim(value, digit, 0, keepdims=False)
        for part in arrived:
            value = value + part.astype(jnp.float32)
    return value.astype(jnp.bfloat16)


def solution(mesh):
    placed = (
        P("sec", None, None),
        P("sec", "mpo", None, None),
        P("sec", "mpo", None, None),
        P("sec", None),
        P("mpo"),
        P("sec", "mpo"),
    )
    return jax.shard_map(
        local, mesh=mesh, in_specs=placed, out_specs=P("sec", "mpo", None), check_vma=False
    )
```

time: 81.8 us -> 26 us (0.32)
  the two profiles are of different devices: /device:TPU:0 before, /device:TPU:8 now
where the time goes in v2:
time: 26 us; the launch traced here: 25.6 us
  starting transfers between devices  8.89 us (34%)
  Pallas kernels  8.54 us (33%)
  waiting for transfers between devices  7.37 us (28%)
  other arithmetic  0.73 us (3%)
    pallas_call x1, Pallas kernels, own(): pl.pallas_call(functools.partial(own_kernel, sectors), in_specs=[HBM, HBM...  4.16 us
    ppermute x3, starting transfers between devices, local(): arrived.append(lax.ppermute(sent, AXES, partners))  3.55 us
    ppermute x1, starting transfers between devices, local(): came = lax.ppermute(sent, AXES, to_core)  3.25 us
    ppermute x3, waiting for transfers between devices, local(): arrived.append(lax.ppermute(sent, AXES, partners))  3.21 us
    ppermute x2, waiting for transfers between devices, local(): lax.ppermute(piece, AXES, halo_pairs(sectors, group))  2.99 us
    ppermute x2, starting transfers between devices, local(): lax.ppermute(piece, AXES, halo_pairs(sectors, group))  2.08 us
    pallas_call x1, Pallas kernels, last(): pl.pallas_call(functools.partial(last_kernel, start), in_specs=[HBM] + [V...  1.61 us
    pallas_call x1, Pallas kernels, shifted(): pl.pallas_call(functools.partial(shifted_kernel, start), in_specs=[VMEM]...  1.51 us
  transfers between devices with their start and end apart: 8, of which 5 were waited for; matrix products, arithmetic and copies ran while one was open for 0% of the time, Pallas kernels for 22%

profile of v2, /device:TPU:8, one launch (start us, length us, event | category | flops | bytes accessed | tf_op | source)
XLA Modules:
  0.0 25.6 jit_solution(10491875998210340164)
XLA Ops:
  0.0 1.3 %shard_map.64 = (bf16[512,256]{1,0:T(8,128)(2,1)S(1)}, bf16[512,256]{1,0:T(8,128)(2,1)S(1)}) custom-call(s32[1,2]{1,0:T(1,128)} %dims_hbm.3, bf16[1,512,512]{2,1,0:T(8,128)(2,1)} %psi_hbm.1), custom_call_target="tpu_custom_call" | custom-call | tf_op jit(solution)/shard_map/pallas_call | solution.py:68
  1.3 0.1 collective-permute-start.2
  1.4 2.0 %collective-permute-start = (bf16[512,256]{1,0:T(8,128)(2,1)S(1)}, bf16[512,256]{1,0:T(8,128)(2,1)S(1)}, u32[]{:S(2)}, u32[]{:S(2)}) collective-permute-start(bf16[512,256]{1,0:T(8,128)(2,1)S(1)} %get-tuple-element.16.refs_1_), channel_id=1, source_target_pairs={{0,8},{1,3},{2,10},{3,1},{4,12},{5,7},{6,14},{7,5},{8,0},{9,17},{1... | collective-permute-start | bytes 786440 | tf_op jit(solution)/shard_map/ppermute | solution.py:223
  3.4 4.2 %shard_map.65 = (f32[512,512]{1,0:T(8,128)S(1)}, bf16[4,512,512]{2,1,0:T(8,128)(2,1)S(1)}, bf16[4,512,512]{2,1,0:T(8,128)(2,1)S(1)}, s32[8,128]{1,0:T(8,128)S(1)}) custom-call(s32[4]{0:T(128)} %shift_hbm.1, s32[1,4]{1,0:T(1,128)} %connect_hbm.1, bf16[512,256]{1,0:T(8,128)(2,1)S(1)} %get-tuple-element.15.refs_0_, ...), custom_call_target="tpu_custom_call" | custom-call | flops 2147483648 | bytes 4194304 | tf_op jit(solution)/shard_map/pallas_call | solution.py:132
  7.5 0.2 collective-permute-done.2.got_ref
  7.7 0.0 collective-permute-start.3
  7.7 2.8 %collective-permute-done.got_ref = bf16[512,256]{1,0:T(8,128)(2,1)S(1)} collective-permute-done((bf16[512,256]{1,0:T(8,128)(2,1)S(1)}, bf16[512,256]{1,0:T(8,128)(2,1)S(1)}, u32[]{:S(2)}, u32[]{:S(2)}) %collective-permute-start) | collective-permute-done | bytes 262176 | tf_op jit(solution)/shard_map/ppermute | solution.py:223
  10.5 0.0 collective-permute-start.1
  10.5 0.0 collective-permute-done.3.swapped_ref
  10.5 1.5 %shard_map.66.before_ref = f32[512,512]{1,0:T(8,128)S(1)} custom-call(s32[8,128]{1,0:T(8,128)S(1)} %get-tuple-element.17.code_ref, bf16[512,256]{1,0:T(8,128)(2,1)S(1)} %collective-permute-done.2.got_ref, bf16[512,256]{1,0:T(8,128)(2,1)S(1)} %collective-permute-done.3.swapped_ref, bf16[4,512,512]{2,1,0:T(8,128)(2,1)S(1)} %get-tuple-element.18.left_ref, ...), custom_call_target="tpu_custom_call" | custom-call | tf_op jit(solution)/shard_map/pallas_call | solution.py:173
  12.0 0.0 collective-permute-done.1.swapped_ref
  12.1 1.6 %shard_map.67 = (f32[4,64,512]{2,1,0:T(8,128)S(1)}, bf16[4,64,512]{2,1,0:T(8,128)(2,1)S(1)}) custom-call(s32[1,2]{1,0:T(1,128)} %dims_hbm.3, s32[8,128]{1,0:T(8,128)S(1)} %get-tuple-element.17.code_ref, bf16[512,256]{1,0:T(8,128)(2,1)S(1)} %collective-permute-done.got_ref, bf16[512,256]{1,0:T(8,128)(2,1)S(1)} %collective-permute-done.1.swapped_ref, ...), custom_call_target="tpu_custom_call" | custom-call | tf_op jit(solution)/shard_map/pallas_call | solution.py:203
  13.7 3.3 %collective-permute-start.4 = (bf16[4,64,512]{2,1,0:T(8,128)(2,1)S(1)}, bf16[4,64,512]{2,1,0:T(8,128)(2,1)S(1)}, u32[]{:S(2)}, u32[]{:S(2)}) collective-permute-start(bf16[4,64,512]{2,1,0:T(8,128)(2,1)S(1)} %get-tuple-element.24), channel_id=1, source_target_pairs={{0,1},{1,0},{2,3},{3,2},{4,5},{5,4},{6,7},{7,6},{8,9},{9,8},{10,11... | collective-permute-start | bytes 786440 | tf_op jit(solution)/shard_map/ppermute | solution.py:233
  16.9 1.2 %collective-permute-done.4 = bf16[4,64,512]{2,1,0:T(8,128)(2,1)S(1)} collective-permute-done((bf16[4,64,512]{2,1,0:T(8,128)(2,1)S(1)}, bf16[4,64,512]{2,1,0:T(8,128)(2,1)S(1)}, u32[]{:S(2)}, u32[]{:S(2)}) %collective-permute-start.4) | collective-permute-done | bytes 262176 | tf_op jit(solution)/shard_map/ppermute | solution.py:233
  18.1 0.1 convert_add_fusion
  18.2 0.1 collective-permute-start.5
  18.3 1.5 %collective-permute-start.6 = (bf16[1,64,512]{2,1,0:T(8,128)(2,1)S(1)}, bf16[1,64,512]{2,1,0:T(8,128)(2,1)S(1)}, u32[]{:S(2)}, u32[]{:S(2)}) collective-permute-start(bf16[1,64,512]{2,1,0:T(8,128)(2,1)S(1)} %get-tuple-element.27), channel_id=1, source_target_pairs={{0,4},{1,3},{2,6},{3,1},{4,0},{5,7},{6,2},{7,5},{8,12},{9,11},{10,... | collective-permute-start | bytes 196616 | tf_op jit(solution)/shard_map/ppermute | solution.py:247
  19.8 2.0 %collective-permute-start.7 = (bf16[1,64,512]{2,1,0:T(8,128)(2,1)S(1)}, bf16[1,64,512]{2,1,0:T(8,128)(2,1)S(1)}, u32[]{:S(2)}, u32[]{:S(2)}) collective-permute-start(bf16[1,64,512]{2,1,0:T(8,128)(2,1)S(1)} %get-tuple-element.26), channel_id=1, source_target_pairs={{0,6},{1,7},{2,4},{3,5},{4,2},{5,3},{6,0},{7,1},{8,14},{9,15},{10,... | collective-permute-start | bytes 196616 | tf_op jit(solution)/shard_map/ppermute | solution.py:247
  21.8 1.3 %collective-permute-done.5 = bf16[1,64,512]{2,1,0:T(8,128)(2,1)S(1)} collective-permute-done((bf16[1,64,512]{2,1,0:T(8,128)(2,1)S(1)}, bf16[1,64,512]{2,1,0:T(8,128)(2,1)S(1)}, u32[]{:S(2)}, u32[]{:S(2)}) %collective-permute-start.5) | collective-permute-done | bytes 65568 | tf_op jit(solution)/shard_map/ppermute | solution.py:247
  23.1 0.0 collective-permute-done.6
  23.1 1.9 %collective-permute-done.7 = bf16[1,64,512]{2,1,0:T(8,128)(2,1)S(1)} collective-permute-done((bf16[1,64,512]{2,1,0:T(8,128)(2,1)S(1)}, bf16[1,64,512]{2,1,0:T(8,128)(2,1)S(1)}, u32[]{:S(2)}, u32[]{:S(2)}) %collective-permute-start.7) | collective-permute-done | bytes 65568 | tf_op jit(solution)/shard_map/ppermute | solution.py:247
  25.0 0.7 %add_convert_fusion = bf16[1,64,512]{2,1,0:T(8,128)(2,1)} fusion(bf16[1,64,512]{2,1,0:T(8,128)(2,1)S(1)} %collective-permute-done.7, bf16[1,64,512]{2,1,0:T(8,128)(2,1)S(1)} %collective-permute-done.6, bf16[1,64,512]{2,1,0:T(8,128)(2,1)S(1)} %collective-permute-done.5, f32[4,64,512]{2,1,0:T(8,128)S(1)} %convert_add_fusion, s32[]{:T(128)S(6)} %select_n.32), kind=kLoop, calls=%fused_computation.1 | loop fusion | flops 229376 | bytes 393220 | tf_op jit(solution)/shard_map/convert_element_type | solution.py:251
  (1 shorter events, 0.0 us)
Async XLA Ops:
  1.3 6.4 %collective-permute-start.2 = (bf16[512,256]{1,0:T(8,128)(2,1)S(1)}, bf16[512,256]{1,0:T(8,128)(2,1)S(1)}, u32[]{:S(2)}, u32[]{:S(2)}) collective-permute-start(bf16[512,256]{1,0:T(8,128)(2,1)S(1)} %get-tuple-element.15.refs_0_), channel_id=1, source_target_pairs={{0,8},{1,3},{2,10},{3,1},{4,12},{5,7},{6,14},{7,5},{8,0},{9,17},{1... | collective-permute-start | bytes 786440 | tf_op jit(solution)/shard_map/ppermute | solution.py:223
  1.4 9.2 %collective-permute-start = (bf16[512,256]{1,0:T(8,128)(2,1)S(1)}, bf16[512,256]{1,0:T(8,128)(2,1)S(1)}, u32[]{:S(2)}, u32[]{:S(2)}) collective-permute-start(bf16[512,256]{1,0:T(8,128)(2,1)S(1)} %get-tuple-element.16.refs_1_), channel_id=1, source_target_pairs={{0,8},{1,3},{2,10},{3,1},{4,12},{5,7},{6,14},{7,5},{8,0},{9,17},{1... | collective-permute-start | bytes 786440 | tf_op jit(solution)/shard_map/ppermute | solution.py:223
  7.7 2.8 %collective-permute-start.3 = (bf16[512,256]{1,0:T(8,128)(2,1)S(1)}, bf16[512,256]{1,0:T(8,128)(2,1)S(1)}, u32[]{:S(2)}, u32[]{:S(2)}) collective-permute-start(bf16[512,256]{1,0:T(8,128)(2,1)S(1)} %collective-permute-done.2.got_ref), channel_id=1, source_target_pairs={{0,1},{1,0},{2,3},{3,2},{4,5},{5,4},{6,7},{7,6},{8,9},{9,8},{10,11... | collective-permute-start | bytes 786440 | tf_op jit(solution)/shard_map/ppermute | solution.py:226
  10.5 1.5 %collective-permute-start.1 = (bf16[512,256]{1,0:T(8,128)(2,1)S(1)}, bf16[512,256]{1,0:T(8,128)(2,1)S(1)}, u32[]{:S(2)}, u32[]{:S(2)}) collective-permute-start(bf16[512,256]{1,0:T(8,128)(2,1)S(1)} %collective-permute-done.got_ref), channel_id=1, source_target_pairs={{0,1},{1,0},{2,3},{3,2},{4,5},{5,4},{6,7},{7,6},{8,9},{9,8},{10,11... | collective-permute-start | bytes 786440 | tf_op jit(solution)/shard_map/ppermute | solution.py:226
  13.7 4.4 %collective-permute-start.4 = (bf16[4,64,512]{2,1,0:T(8,128)(2,1)S(1)}, bf16[4,64,512]{2,1,0:T(8,128)(2,1)S(1)}, u32[]{:S(2)}, u32[]{:S(2)}) collective-permute-start(bf16[4,64,512]{2,1,0:T(8,128)(2,1)S(1)} %get-tuple-element.24), channel_id=1, source_target_pairs={{0,1},{1,0},{2,3},{3,2},{4,5},{5,4},{6,7},{7,6},{8,9},{9,8},{10,11... | collective-permute-start | bytes 786440 | tf_op jit(solution)/shard_map/ppermute | solution.py:233
  18.2 4.9 %collective-permute-start.5 = (bf16[1,64,512]{2,1,0:T(8,128)(2,1)S(1)}, bf16[1,64,512]{2,1,0:T(8,128)(2,1)S(1)}, u32[]{:S(2)}, u32[]{:S(2)}) collective-permute-start(bf16[1,64,512]{2,1,0:T(8,128)(2,1)S(1)} %get-tuple-element.25), channel_id=1, source_target_pairs={{0,2},{1,5},{2,0},{3,7},{4,6},{5,1},{6,4},{7,3},{8,10},{9,13},{10,... | collective-permute-start | bytes 196616 | tf_op jit(solution)/shard_map/ppermute | solution.py:247
  18.3 4.8 %collective-permute-start.6 = (bf16[1,64,512]{2,1,0:T(8,128)(2,1)S(1)}, bf16[1,64,512]{2,1,0:T(8,128)(2,1)S(1)}, u32[]{:S(2)}, u32[]{:S(2)}) collective-permute-start(bf16[1,64,512]{2,1,0:T(8,128)(2,1)S(1)} %get-tuple-element.27), channel_id=1, source_target_pairs={{0,4},{1,3},{2,6},{3,1},{4,0},{5,7},{6,2},{7,5},{8,12},{9,11},{10,... | collective-permute-start | bytes 196616 | tf_op jit(solution)/shard_map/ppermute | solution.py:247
  19.8 5.2 %collective-permute-start.7 = (bf16[1,64,512]{2,1,0:T(8,128)(2,1)S(1)}, bf16[1,64,512]{2,1,0:T(8,128)(2,1)S(1)}, u32[]{:S(2)}, u32[]{:S(2)}) collective-permute-start(bf16[1,64,512]{2,1,0:T(8,128)(2,1)S(1)} %get-tuple-element.26), channel_id=1, source_target_pairs={{0,6},{1,7},{2,4},{3,5},{4,2},{5,3},{6,0},{7,1},{8,14},{9,15},{10,... | collective-permute-start | bytes 196616 | tf_op jit(solution)/shard_map/ppermute | solution.py:247

commit v3 on v2

v3 whole, which is shorter than its diff:
```python
import functools

import jax
import jax.numpy as jnp
from jax import lax
from jax.experimental import pallas as pl
from jax.experimental.pallas import tpu as pltpu
from jax.sharding import PartitionSpec as P

AXES = ("sec", "mpo")
CUTS = (256, 256)
VMEM = pl.BlockSpec(memory_space=pltpu.VMEM)
HBM = pl.BlockSpec(memory_space=pltpu.HBM)
PARAMS = pltpu.CompilerParams(vmem_limit_bytes=8 * 1024 * 1024)


def halo_pairs(sectors, group):
    pairs = []
    for sector in range(sectors):
        for place in range(group):
            there = sector + 1 if (sector + place) % 2 == 0 else sector - 1
            if 0 <= there < sectors:
                pairs.append((sector * group + place, there * group + place))
            elif group % 4 == 0:
                pairs.append((sector * group + place, sector * group + (place ^ 2)))
    return pairs


def group_pairs(sectors, group, flip_of):
    return [
        (sector * group + place, sector * group + (place ^ flip_of(place % 2)))
        for sector in range(sectors)
        for place in range(group)
    ]


def in_hbm(array):
    return pltpu.with_memory_space_constraint(array, pltpu.HBM)


def dot(a, b):
    return jnp.dot(a, b, preferred_element_type=jnp.float32)


def mask_kernel(dims_hbm, psi_hbm, *refs):
    *out_refs, dims_ref, psi_ref, sems = refs
    copies = [
        pltpu.make_async_copy(dims_hbm, dims_ref, sems.at[0]),
        pltpu.make_async_copy(psi_hbm.at[0], psi_ref, sems.at[1]),
    ]
    for copy in copies:
        copy.start()
    for copy in copies:
        copy.wait()
    start = 0
    for out_ref in out_refs:
        shape = out_ref.shape
        rows = lax.broadcasted_iota(jnp.int32, shape, 0)
        cols = lax.broadcasted_iota(jnp.int32, shape, 1) + start
        keep = (rows < dims_ref[0, 0] * 32) & (cols < dims_ref[0, 1] * 32)
        piece = psi_ref[:, start : start + shape[1]]
        out_ref[...] = jnp.where(keep, piece, jnp.zeros_like(piece))
        start += shape[1]


def mask(dims, psi):
    order = psi.shape[1]
    return pl.pallas_call(
        mask_kernel,
        in_specs=[HBM, HBM],
        out_specs=[VMEM] * len(CUTS),
        out_shape=[jax.ShapeDtypeStruct((order, cut), jnp.bfloat16) for cut in CUTS],
        scratch_shapes=[
            pltpu.SMEM(dims.shape, jnp.int32),
            pltpu.VMEM(psi.shape[1:], psi.dtype),
            pltpu.SemaphoreType.DMA((2,)),
        ],
        compiler_params=PARAMS,
    )(in_hbm(dims), in_hbm(psi))


def load_kernel(sectors, dims_hbm, shift_hbm, connect_hbm, left_hbm, right_hbm, left_ref, right_ref, code_ref, keep_ref, dims_ref, shift_ref, connect_ref, sems):
    terms = left_ref.shape[0]
    scalars = [(dims_hbm, dims_ref), (shift_hbm, shift_ref), (connect_hbm, connect_ref)]
    copies = [pltpu.make_async_copy(a, b, sems.at[at]) for at, (a, b) in enumerate(scalars)]
    for term in range(terms):
        for which, (a, b) in enumerate(((left_hbm, left_ref), (right_hbm, right_ref))):
            copies.append(pltpu.make_async_copy(a.at[0, term], b.at[term], sems.at[len(copies)]))
    for copy in copies:
        copy.start()
    for copy in copies[:3]:
        copy.wait()

    sector, place = lax.axis_index("sec"), lax.axis_index("mpo")
    above = (sector + place) % 2 == 0
    code = jnp.int32(0)
    for term in range(terms):
        shift = shift_ref[term]
        there = sector - shift
        used = (connect_ref[0, term] != 0) & (there >= 0) & (there < sectors)
        direct = (shift < 0) == above
        choice = jnp.where(shift == 0, 3, jnp.where(direct, 2, 1))
        code += jnp.where(used, choice, 0) << (2 * term)
    code_ref[...] = jnp.full(code_ref.shape, code, jnp.int32)

    rows = lax.broadcasted_iota(jnp.int32, keep_ref.shape, 0) + place * keep_ref.shape[0]
    cols = lax.broadcasted_iota(jnp.int32, keep_ref.shape, 1)
    keep = (rows < dims_ref[0, 0] * 32) & (cols < dims_ref[0, 1] * 32)
    keep_ref[...] = jnp.where(keep, 1.0, 0.0)
    for copy in copies[3:]:
        copy.wait()


def load(sectors, group, dims, term_shift, connect, left, right):
    _, terms, order, _ = left.shape
    return pl.pallas_call(
        functools.partial(load_kernel, sectors),
        in_specs=[HBM] * 5,
        out_specs=[VMEM] * 4,
        out_shape=[
            pltpu.VMEM(left.shape[1:], left.dtype),
            pltpu.VMEM(right.shape[1:], right.dtype),
            pltpu.VMEM((8, 128), jnp.int32),
            pltpu.VMEM((order // group, order), jnp.float32),
        ],
        scratch_shapes=[
            pltpu.SMEM(dims.shape, jnp.int32),
            pltpu.SMEM(term_shift.shape, jnp.int32),
            pltpu.SMEM(connect.shape, jnp.int32),
            pltpu.SemaphoreType.DMA((2 * terms + 3,)),
        ],
        compiler_params=PARAMS,
        cost_estimate=pl.CostEstimate(flops=4 * terms * order**3, bytes_accessed=4 * terms * order**2, transcendentals=0),
    )(*[in_hbm(array) for array in (dims, term_shift, connect, left, right)])


def products(start, rows_of, code_ref, own_ref, got_ref, swapped_ref, left_ref, right_ref, first_ref):
    code = code_ref[0, 0]
    terms, order, _ = right_ref.shape
    width = own_ref.shape[1]
    for term in range(terms):
        choice = (code >> (2 * term)) & 3
        own, got, swapped = own_ref[...], got_ref[...], swapped_ref[...]
        source = jnp.where(choice == 3, own, jnp.where(choice == 2, got, jnp.where(choice == 1, swapped, jnp.zeros_like(own))))
        first_ref[:, term * width : (term + 1) * width] = dot(rows_of(left_ref, term), source).astype(jnp.bfloat16)
    right = right_ref[:, start : start + width, :].reshape(terms * width, order)
    return dot(first_ref[...], right)


def part_kernel(start, code_ref, own_ref, got_ref, swapped_ref, left_ref, right_ref, *refs):
    *before, total_ref, first_ref = refs
    total = products(start, lambda left, term: left[term], code_ref, own_ref, got_ref, swapped_ref, left_ref, right_ref, first_ref)
    for ref in before:
        total += ref[...]
    total_ref[...] = total


def part(start, code, own, got, swapped, left, right, before):
    terms, order, _ = left.shape
    operands = [code, own, got, swapped, left, right, *before]
    return pl.pallas_call(
        functools.partial(part_kernel, start),
        in_specs=[VMEM] * len(operands),
        out_specs=VMEM,
        out_shape=pltpu.VMEM((order, order), jnp.float32),
        scratch_shapes=[pltpu.VMEM((order, terms * own.shape[1]), jnp.bfloat16)],
        compiler_params=PARAMS,
    )(*operands)


def half_kernel(start, theirs, code_ref, own_ref, got_ref, swapped_ref, left_ref, right_ref, before_ref, out_ref, first_ref):
    blocks, height, _ = out_ref.shape
    core = lax.axis_index("mpo") % 2
    side = 1 - core if theirs else core
    places = [pl.ds(pl.multiple_of((2 * block + side) * height, height), height) for block in range(blocks)]

    def rows_of(left, term):
        return jnp.concatenate([left[term, at] for at in places], axis=0)

    total = products(start, rows_of, code_ref, own_ref, got_ref, swapped_ref, left_ref, right_ref, first_ref)
    for block, at in enumerate(places):
        value = total[block * height : (block + 1) * height] + before_ref[at]
        out_ref[block] = value.astype(out_ref.dtype)


def half(start, theirs, group, code, own, got, swapped, left, right, before):
    terms, order, _ = left.shape
    return pl.pallas_call(
        functools.partial(half_kernel, start, theirs),
        in_specs=[VMEM] * 7,
        out_specs=VMEM,
        out_shape=pltpu.VMEM((group // 2, order // group, order), jnp.bfloat16 if theirs else jnp.float32),
        scratch_shapes=[pltpu.VMEM((order // 2, terms * own.shape[1]), jnp.bfloat16)],
        compiler_params=PARAMS,
        cost_estimate=pl.CostEstimate(flops=2 * terms * order**2 * own.shape[1], bytes_accessed=0, transcendentals=0),
    )(code, own, got, swapped, left, right, before)


def split_kernel(shift, flips, *refs):
    ways = 1 + len(flips[0])
    *addends, own_ref = refs[: len(refs) - ways + 1]
    send_refs = refs[len(refs) - ways + 1 :]
    count = own_ref.shape[0]
    place = lax.axis_index("mpo")
    digit = (place >> shift) & (ways - 1)

    def summed(block):
        value = addends[0][block]
        for other in addends[1:]:
            value += other[block].astype(jnp.float32)
        return value

    for ref, even, odd in zip(send_refs, *flips):
        flip = jnp.where(place % 2 == 0, even, odd)
        for at in range(count):
            ref[at] = summed((digit ^ flip) * count + at).astype(ref.dtype)
    for at in range(count):
        own_ref[at] = summed(digit * count + at)


def split(addends, shift, flips):
    ways = 1 + len(flips[0])
    blocks, height, width = addends[0].shape
    shape = (blocks // ways, height, width)
    own, *sends = pl.pallas_call(
        functools.partial(split_kernel, shift, flips),
        in_specs=[VMEM] * len(addends),
        out_specs=[VMEM] * ways,
        out_shape=[pltpu.VMEM(shape, jnp.float32)] + [pltpu.VMEM(shape, jnp.bfloat16)] * (ways - 1),
        compiler_params=PARAMS,
    )(*addends)
    return sends, own


def local(psi, left_env, right_env, dims, term_shift, connect):
    sectors, group = lax.axis_size("sec"), lax.axis_size("mpo")
    place = lax.axis_index("mpo")
    order = psi.shape[1]

    pieces = mask(dims, psi)
    to_core = group_pairs(sectors, group, lambda core: 1)
    got = [lax.ppermute(piece, AXES, halo_pairs(sectors, group)) for piece in pieces]
    left, right, code, keep = load(sectors, group, dims, term_shift, connect, left_env, right_env)
    got[0], code = lax.optimization_barrier((got[0], code))
    swapped = [lax.ppermute(piece, AXES, to_core) for piece in got]
    start, total = 0, []
    for at in range(len(CUTS) - 1):
        total = [part(start, code, pieces[at], got[at], swapped[at], left, right, total)]
        start += CUTS[at]
    last = (code, pieces[-1], got[-1], swapped[-1], left, right)
    if (order // group) % 16 == 0:
        sent = half(start, True, group, *last, *total)
        kept = half(start, False, group, *last, *total)
    else:
        blocks = part(start, *last, total).reshape(group // 2, 2, order // group, order)
        kept = lax.dynamic_index_in_dim(blocks, place % 2, 1, keepdims=False)
        sent = lax.dynamic_index_in_dim(blocks, 1 - place % 2, 1, keepdims=False).astype(jnp.bfloat16)

    addends = [kept, lax.ppermute(sent, AXES, to_core)]
    bits = (group // 2).bit_length() - 1
    while bits:
        taken = min(bits, 2)
        bits -= taken
        flips = [(1, 2, 3), (2, 1, 3)] if taken == 2 else [(1,), (1,)]
        sends, own = split(addends, 1 + bits, flips)
        addends = [own]
        for sent, even, odd in zip(sends, *flips):
            partners = group_pairs(sectors, group, lambda core: (odd if core else even) << (1 + bits))
            addends.append(lax.ppermute(sent, AXES, partners))
    value = addends[0]
    for other in addends[1:]:
        value = value + other.astype(jnp.float32)
    value = jnp.where(keep != 0, value.reshape(keep.shape), 0.0)
    return value.astype(jnp.bfloat16)[None]


def solution(mesh):
    placed = (
        P("sec", None, None),
        P("sec", "mpo", None, None),
        P("sec", "mpo", None, None),
        P("sec", None),
        P("mpo"),
        P("sec", "mpo"),
    )
    return jax.shard_map(
        local, mesh=mesh, in_specs=placed, out_specs=P("sec", "mpo", None), check_vma=False
    )
```

time: 26 us -> 25 us (0.962)
  the two profiles are of different devices: /device:TPU:8 before, /device:TPU:0 now
where the time goes in v3:
time: 25 us; the launch traced here: 24.8 us
  waiting for transfers between devices  10.7 us (43%)
  starting transfers between devices  7.09 us (28%)
  Pallas kernels  6.37 us (25%)
  other arithmetic  0.67 us (3%)
    ppermute x3, waiting for transfers between devices, local(): addends.append(lax.ppermute(sent, AXES, partners))  5.13 us
    ppermute x2, waiting for transfers between devices, local(): lax.ppermute(piece, AXES, halo_pairs(sectors, group))  4.83 us
    ppermute x3, starting transfers between devices, local(): addends.append(lax.ppermute(sent, AXES, partners))  3.55 us
    ppermute x2, starting transfers between devices, local(): lax.ppermute(piece, AXES, halo_pairs(sectors, group))  3.17 us
    pallas_call x1, Pallas kernels, load(): pl.pallas_call(functools.partial(load_kernel, sectors), in_specs=[HBM] *...  2.24 us
    pallas_call x2, Pallas kernels, half(): pl.pallas_call(functools.partial(half_kernel, start, theirs), in_specs=[V...  1.51 us
    pallas_call x1, Pallas kernels, part(): pl.pallas_call(functools.partial(part_kernel, start), in_specs=[VMEM] * l...  1.3 us
    pallas_call x1, Pallas kernels, mask(): pl.pallas_call(mask_kernel, in_specs=[HBM, HBM], out_specs=[VMEM] * len(C...  1.27 us
  transfers between devices with their start and end apart: 8, of which 7 were waited for; matrix products, arithmetic and copies ran while one was open for 0% of the time, Pallas kernels for 17%

profile of v3, /device:TPU:0, one launch (start us, length us, event | category | flops | bytes accessed | tf_op | source)
XLA Modules:
  0.0 24.8 jit_solution(6391478772944799949)
XLA Ops:
  0.0 1.3 %shard_map.65 = (bf16[512,256]{1,0:T(8,128)(2,1)S(1)}, bf16[512,256]{1,0:T(8,128)(2,1)S(1)}) custom-call(s32[1,2]{1,0:T(1,128)} %dims_hbm.3, bf16[1,512,512]{2,1,0:T(8,128)(2,1)} %psi_hbm.1), custom_call_target="tpu_custom_call" | custom-call | tf_op jit(solution)/shard_map/pallas_call | solution.py:68
  1.3 3.1 %collective-permute-start = (bf16[512,256]{1,0:T(8,128)(2,1)S(1)}, bf16[512,256]{1,0:T(8,128)(2,1)S(1)}, u32[]{:S(2)}, u32[]{:S(2)}) collective-permute-start(bf16[512,256]{1,0:T(8,128)(2,1)S(1)} %get-tuple-element.18.own_ref), channel_id=1, source_target_pairs={{0,8},{1,3},{2,10},{3,1},{4,12},{5,7},{6,14},{7,5},{8,0},{9,17},{1... | collective-permute-start | bytes 786440 | tf_op jit(solution)/shard_map/ppermute | solution.py:242
  4.4 0.1 collective-permute-start.1
  4.4 2.2 %shard_map.64 = (bf16[4,512,512]{2,1,0:T(8,128)(2,1)S(1)}, bf16[4,512,512]{2,1,0:T(8,128)(2,1)S(1)}, s32[8,128]{1,0:T(8,128)S(1)}, f32[64,512]{1,0:T(8,128)S(1)}) custom-call(s32[1,2]{1,0:T(1,128)} %dims_hbm.3, s32[4]{0:T(128)} %shift_hbm.1, s32[1,4]{1,0:T(1,128)} %connect_hbm.1, bf16[1,4,512,512]{3,2,1,0:T(8,128)(2,1)} %left_hbm.1, ...), custom_call_target="tpu_custom_call" | custom-call | flops 2147483648 | bytes 4194304 | tf_op jit(solution)/shard_map/pallas_call | solution.py:116
  6.7 2.0 %collective-permute-done.got_ref = bf16[512,256]{1,0:T(8,128)(2,1)S(1)} collective-permute-done((bf16[512,256]{1,0:T(8,128)(2,1)S(1)}, bf16[512,256]{1,0:T(8,128)(2,1)S(1)}, u32[]{:S(2)}, u32[]{:S(2)}) %collective-permute-start) | collective-permute-done | bytes 262176 | tf_op jit(solution)/shard_map/ppermute | solution.py:242
  8.7 0.0 collective-permute-start.3
  8.7 2.8 %collective-permute-done.1.got_ref = bf16[512,256]{1,0:T(8,128)(2,1)S(1)} collective-permute-done((bf16[512,256]{1,0:T(8,128)(2,1)S(1)}, bf16[512,256]{1,0:T(8,128)(2,1)S(1)}, u32[]{:S(2)}, u32[]{:S(2)}) %collective-permute-start.1) | collective-permute-done | bytes 262176 | tf_op jit(solution)/shard_map/ppermute | solution.py:242
  11.5 0.0 collective-permute-start.2
  11.5 0.0 collective-permute-done.3.swapped_ref
  11.5 1.3 %shard_map.66.before_ref = f32[512,512]{1,0:T(8,128)S(1)} custom-call(s32[8,128]{1,0:T(8,128)S(1)} %get-tuple-element.20.code_ref, bf16[512,256]{1,0:T(8,128)(2,1)S(1)} %get-tuple-element.18.own_ref, bf16[512,256]{1,0:T(8,128)(2,1)S(1)} %collective-permute-done.got_ref, bf16[512,256]{1,0:T(8,128)(2,1)S(1)} %collective-permute-done.3.swapped_ref, ...), custom_call_target="tpu_custom_call" | custom-call | tf_op jit(solution)/shard_map/pallas_call | solution.py:161
  12.8 0.2 collective-permute-done.2.swapped_ref
  13.1 0.8 %shard_map.68 = bf16[4,64,512]{2,1,0:T(8,128)(2,1)S(1)} custom-call(s32[8,128]{1,0:T(8,128)S(1)} %get-tuple-element.20.code_ref, bf16[512,256]{1,0:T(8,128)(2,1)S(1)} %get-tuple-element.21.own_ref, bf16[512,256]{1,0:T(8,128)(2,1)S(1)} %collective-permute-done.1.got_ref, bf16[512,256]{1,0:T(8,128)(2,1)S(1)} %collective-permute-done.2.swapped_ref, ...), custom_call_target="tpu_custom_call" | custom-call | flops 536870912 | tf_op jit(solution)/shard_map/pallas_call | solution.py:188
  13.8 0.4 %collective-permute-start.4 = (bf16[4,64,512]{2,1,0:T(8,128)(2,1)S(1)}, bf16[4,64,512]{2,1,0:T(8,128)(2,1)S(1)}, u32[]{:S(2)}, u32[]{:S(2)}) collective-permute-start(bf16[4,64,512]{2,1,0:T(8,128)(2,1)S(1)} %shard_map.68), channel_id=1, source_target_pairs={{0,1},{1,0},{2,3},{3,2},{4,5},{5,4},{6,7},{7,6},{8,9},{9,8},{10,11... | collective-permute-start | bytes 786440 | tf_op jit(solution)/shard_map/ppermute | solution.py:259
  14.2 0.8 %shard_map.67.refs_0_ = f32[4,64,512]{2,1,0:T(8,128)S(1)} custom-call(s32[8,128]{1,0:T(8,128)S(1)} %get-tuple-element.20.code_ref, bf16[512,256]{1,0:T(8,128)(2,1)S(1)} %get-tuple-element.21.own_ref, bf16[512,256]{1,0:T(8,128)(2,1)S(1)} %collective-permute-done.1.got_ref, bf16[512,256]{1,0:T(8,128)(2,1)S(1)} %collective-permute-done.2.swapped_ref, ...), custom_call_target="tpu_custom_call" | custom-call | flops 536870912 | tf_op jit(solution)/shard_map/pallas_call | solution.py:188
  14.9 0.5 %collective-permute-done.4.refs_1_ = bf16[4,64,512]{2,1,0:T(8,128)(2,1)S(1)} collective-permute-done((bf16[4,64,512]{2,1,0:T(8,128)(2,1)S(1)}, bf16[4,64,512]{2,1,0:T(8,128)(2,1)S(1)}, u32[]{:S(2)}, u32[]{:S(2)}) %collective-permute-start.4) | collective-permute-done | bytes 262176 | tf_op jit(solution)/shard_map/ppermute | solution.py:259
  15.5 2.0 %collective-permute-start.5 = (bf16[1,64,512]{2,1,0:T(8,128)(2,1)S(1)}, bf16[1,64,512]{2,1,0:T(8,128)(2,1)S(1)}, u32[]{:S(2)}, u32[]{:S(2)}) collective-permute-start(bf16[1,64,512]{2,1,0:T(8,128)(2,1)S(1)} %get-tuple-element.26), channel_id=1, source_target_pairs={{0,2},{1,5},{2,0},{3,7},{4,6},{5,1},{6,4},{7,3},{8,10},{9,13},{10,... | collective-permute-start | bytes 196616 | tf_op jit(solution)/shard_map/ppermute | solution.py:269
  17.5 1.5 %collective-permute-start.6 = (bf16[1,64,512]{2,1,0:T(8,128)(2,1)S(1)}, bf16[1,64,512]{2,1,0:T(8,128)(2,1)S(1)}, u32[]{:S(2)}, u32[]{:S(2)}) collective-permute-start(bf16[1,64,512]{2,1,0:T(8,128)(2,1)S(1)} %get-tuple-element.27), channel_id=1, source_target_pairs={{0,4},{1,3},{2,6},{3,1},{4,0},{5,7},{6,2},{7,5},{8,12},{9,11},{10,... | collective-permute-start | bytes 196616 | tf_op jit(solution)/shard_map/ppermute | solution.py:269
  19.0 0.0 collective-permute-start.7
  19.0 0.8 %collective-permute-done.5 = bf16[1,64,512]{2,1,0:T(8,128)(2,1)S(1)} collective-permute-done((bf16[1,64,512]{2,1,0:T(8,128)(2,1)S(1)}, bf16[1,64,512]{2,1,0:T(8,128)(2,1)S(1)}, u32[]{:S(2)}, u32[]{:S(2)}) %collective-permute-start.5) | collective-permute-done | bytes 65568 | tf_op jit(solution)/shard_map/ppermute | solution.py:269
  19.8 1.9 %collective-permute-done.6 = bf16[1,64,512]{2,1,0:T(8,128)(2,1)S(1)} collective-permute-done((bf16[1,64,512]{2,1,0:T(8,128)(2,1)S(1)}, bf16[1,64,512]{2,1,0:T(8,128)(2,1)S(1)}, u32[]{:S(2)}, u32[]{:S(2)}) %collective-permute-start.6) | collective-permute-done | bytes 65568 | tf_op jit(solution)/shard_map/ppermute | solution.py:269
  21.7 2.4 %collective-permute-done.7 = bf16[1,64,512]{2,1,0:T(8,128)(2,1)S(1)} collective-permute-done((bf16[1,64,512]{2,1,0:T(8,128)(2,1)S(1)}, bf16[1,64,512]{2,1,0:T(8,128)(2,1)S(1)}, u32[]{:S(2)}, u32[]{:S(2)}) %collective-permute-start.7) | collective-permute-done | bytes 65568 | tf_op jit(solution)/shard_map/ppermute | solution.py:269
  24.2 0.7 %fusion.1 = bf16[1,64,512]{2,1,0:T(8,128)(2,1)} fusion(bf16[1,64,512]{2,1,0:T(8,128)(2,1)S(1)} %collective-permute-done.7, bf16[1,64,512]{2,1,0:T(8,128)(2,1)S(1)} %collective-permute-done.6, f32[1,64,512]{2,1,0:T(8,128)S(1)} %get-tuple-element.25, bf16[1,64,512]{2,1,0:T(8,128)(2,1)S(1)} %collective-permute-done.5, f32[64,512]{1,0:T(8,128)S(1)} %get-tuple-element.17), kind=kLoop, calls=%fused_computation.2 | loop fusion | flops 294912 | bytes 524288 | tf_op jit(solution)/shard_map/broadcast_in_dim | solution.py:274
  (1 shorter events, 0.0 us)
Async XLA Ops:
  1.3 7.4 %collective-permute-start = (bf16[512,256]{1,0:T(8,128)(2,1)S(1)}, bf16[512,256]{1,0:T(8,128)(2,1)S(1)}, u32[]{:S(2)}, u32[]{:S(2)}) collective-permute-start(bf16[512,256]{1,0:T(8,128)(2,1)S(1)} %get-tuple-element.18.own_ref), channel_id=1, source_target_pairs={{0,8},{1,3},{2,10},{3,1},{4,12},{5,7},{6,14},{7,5},{8,0},{9,17},{1... | collective-permute-start | bytes 786440 | tf_op jit(solution)/shard_map/ppermute | solution.py:242
  4.4 7.2 %collective-permute-start.1 = (bf16[512,256]{1,0:T(8,128)(2,1)S(1)}, bf16[512,256]{1,0:T(8,128)(2,1)S(1)}, u32[]{:S(2)}, u32[]{:S(2)}) collective-permute-start(bf16[512,256]{1,0:T(8,128)(2,1)S(1)} %get-tuple-element.21.own_ref), channel_id=1, source_target_pairs={{0,8},{1,3},{2,10},{3,1},{4,12},{5,7},{6,14},{7,5},{8,0},{9,17},{1... | collective-permute-start | bytes 786440 | tf_op jit(solution)/shard_map/ppermute | solution.py:242
  8.7 2.8 %collective-permute-start.3 = (bf16[512,256]{1,0:T(8,128)(2,1)S(1)}, bf16[512,256]{1,0:T(8,128)(2,1)S(1)}, u32[]{:S(2)}, u32[]{:S(2)}) collective-permute-start(bf16[512,256]{1,0:T(8,128)(2,1)S(1)} %collective-permute-done.got_ref), channel_id=1, source_target_pairs={{0,1},{1,0},{2,3},{3,2},{4,5},{5,4},{6,7},{7,6},{8,9},{9,8},{10,11... | collective-permute-start | bytes 786440 | tf_op jit(solution)/shard_map/ppermute | solution.py:245
  11.5 1.5 %collective-permute-start.2 = (bf16[512,256]{1,0:T(8,128)(2,1)S(1)}, bf16[512,256]{1,0:T(8,128)(2,1)S(1)}, u32[]{:S(2)}, u32[]{:S(2)}) collective-permute-start(bf16[512,256]{1,0:T(8,128)(2,1)S(1)} %collective-permute-done.1.got_ref), channel_id=1, source_target_pairs={{0,1},{1,0},{2,3},{3,2},{4,5},{5,4},{6,7},{7,6},{8,9},{9,8},{10,11... | collective-permute-start | bytes 786440 | tf_op jit(solution)/shard_map/ppermute | solution.py:245
  13.8 1.6 %collective-permute-start.4 = (bf16[4,64,512]{2,1,0:T(8,128)(2,1)S(1)}, bf16[4,64,512]{2,1,0:T(8,128)(2,1)S(1)}, u32[]{:S(2)}, u32[]{:S(2)}) collective-permute-start(bf16[4,64,512]{2,1,0:T(8,128)(2,1)S(1)} %shard_map.68), channel_id=1, source_target_pairs={{0,1},{1,0},{2,3},{3,2},{4,5},{5,4},{6,7},{7,6},{8,9},{9,8},{10,11... | collective-permute-start | bytes 786440 | tf_op jit(solution)/shard_map/ppermute | solution.py:259
  15.5 4.3 %collective-permute-start.5 = (bf16[1,64,512]{2,1,0:T(8,128)(2,1)S(1)}, bf16[1,64,512]{2,1,0:T(8,128)(2,1)S(1)}, u32[]{:S(2)}, u32[]{:S(2)}) collective-permute-start(bf16[1,64,512]{2,1,0:T(8,128)(2,1)S(1)} %get-tuple-element.26), channel_id=1, source_target_pairs={{0,2},{1,5},{2,0},{3,7},{4,6},{5,1},{6,4},{7,3},{8,10},{9,13},{10,... | collective-permute-start | bytes 196616 | tf_op jit(solution)/shard_map/ppermute | solution.py:269
  17.5 4.3 %collective-permute-start.6 = (bf16[1,64,512]{2,1,0:T(8,128)(2,1)S(1)}, bf16[1,64,512]{2,1,0:T(8,128)(2,1)S(1)}, u32[]{:S(2)}, u32[]{:S(2)}) collective-permute-start(bf16[1,64,512]{2,1,0:T(8,128)(2,1)S(1)} %get-tuple-element.27), channel_id=1, source_target_pairs={{0,4},{1,3},{2,6},{3,1},{4,0},{5,7},{6,2},{7,5},{8,12},{9,11},{10,... | collective-permute-start | bytes 196616 | tf_op jit(solution)/shard_map/ppermute | solution.py:269
  19.0 5.2 %collective-permute-start.7 = (bf16[1,64,512]{2,1,0:T(8,128)(2,1)S(1)}, bf16[1,64,512]{2,1,0:T(8,128)(2,1)S(1)}, u32[]{:S(2)}, u32[]{:S(2)}) collective-permute-start(bf16[1,64,512]{2,1,0:T(8,128)(2,1)S(1)} %get-tuple-element.28), channel_id=1, source_target_pairs={{0,6},{1,7},{2,4},{3,5},{4,2},{5,3},{6,0},{7,1},{8,14},{9,15},{10,... | collective-permute-start | bytes 196616 | tf_op jit(solution)/shard_map/ppermute | solution.py:269

commit v4 on v3

--- a/solution.py
+++ b/solution.py
@@ -9,6 +9,7 @@
 
 AXES = ("sec", "mpo")
 CUTS = (256, 256)
+FLIPS = {4: (3, 1, 2), 2: (1,)}
 VMEM = pl.BlockSpec(memory_space=pltpu.VMEM)
 HBM = pl.BlockSpec(memory_space=pltpu.HBM)
 PARAMS = pltpu.CompilerParams(vmem_limit_bytes=8 * 1024 * 1024)
@@ -18,20 +19,36 @@
     pairs = []
     for sector in range(sectors):
         for place in range(group):
-            there = sector + 1 if (sector + place) % 2 == 0 else sector - 1
+            there = sector + 1 if place % 2 == 0 else sector - 1
             if 0 <= there < sectors:
-                pairs.append((sector * group + place, there * group + place))
+                pairs.append((sector * group + place, there * group + (place ^ 1)))
             elif group % 4 == 0:
                 pairs.append((sector * group + place, sector * group + (place ^ 2)))
     return pairs
 
 
-def group_pairs(sectors, group, flip_of):
+def group_pairs(sectors, group, flip):
     return [
-        (sector * group + place, sector * group + (place ^ flip_of(place % 2)))
+        (sector * group + place, sector * group + (place ^ flip))
         for sector in range(sectors)
         for place in range(group)
     ]
+
+
+def stages_of(group):
+    bits, stages = (group // 2).bit_length() - 1, []
+    while bits:
+        taken = min(bits, 2)
+        bits -= taken
+        stages.append((bits, 1 << taken))
+    return stages
+
+
+def core_for(group, place, chip):
+    core, differ = place % 2, (place // 2) ^ chip
+    for bit, ways in stages_of(group):
+        core = core ^ jnp.where((differ >> bit) & (ways - 1) != 0, 1, 0)
+    return core
 
 
 def in_hbm(array):
@@ -92,7 +109,7 @@
         copy.wait()
 
     sector, place = lax.axis_index("sec"), lax.axis_index("mpo")
-    above = (sector + place) % 2 == 0
+    above = place % 2 == 0
     code = jnp.int32(0)
     for term in range(terms):
         shift = shift_ref[term]
@@ -168,11 +185,18 @@
     )(*operands)
 
 
-def half_kernel(start, theirs, code_ref, own_ref, got_ref, swapped_ref, left_ref, right_ref, before_ref, out_ref, first_ref):
-    blocks, height, _ = out_ref.shape
-    core = lax.axis_index("mpo") % 2
-    side = 1 - core if theirs else core
-    places = [pl.ds(pl.multiple_of((2 * block + side) * height, height), height) for block in range(blocks)]
+def row_blocks(group, height, theirs):
+    place = lax.axis_index("mpo")
+    firsts = []
+    for chip in range(group // 2):
+        core = core_for(group, place, chip)
+        firsts.append((2 * chip + (1 - core if theirs else core)) * height)
+    return [pl.ds(pl.multiple_of(first, height), height) for first in firsts]
+
+
+def half_kernel(start, theirs, group, code_ref, own_ref, got_ref, swapped_ref, left_ref, right_ref, before_ref, out_ref, first_ref):
+    height = out_ref.shape[1]
+    places = row_blocks(group, height, theirs)
 
     def rows_of(left, term):
         return jnp.concatenate([left[term, at] for at in places], axis=0)
@@ -186,7 +210,7 @@
 def half(start, theirs, group, code, own, got, swapped, left, right, before):
     terms, order, _ = left.shape
     return pl.pallas_call(
-        functools.partial(half_kernel, start, theirs),
+        functools.partial(half_kernel, start, theirs, group),
         in_specs=[VMEM] * 7,
         out_specs=VMEM,
         out_shape=pltpu.VMEM((group // 2, order // group, order), jnp.bfloat16 if theirs else jnp.float32),
@@ -196,13 +220,30 @@
     )(code, own, got, swapped, left, right, before)
 
 
-def split_kernel(shift, flips, *refs):
-    ways = 1 + len(flips[0])
+def pick_kernel(group, total_ref, sent_ref, kept_ref):
+    for out_ref, theirs in ((sent_ref, True), (kept_ref, False)):
+        for block, at in enumerate(row_blocks(group, out_ref.shape[1], theirs)):
+            out_ref[block] = total_ref[at].astype(out_ref.dtype)
+
+
+def pick(group, total):
+    order = total.shape[0]
+    shape = (group // 2, order // group, order)
+    return pl.pallas_call(
+        functools.partial(pick_kernel, group),
+        in_specs=[VMEM],
+        out_specs=[VMEM, VMEM],
+        out_shape=[pltpu.VMEM(shape, jnp.bfloat16), pltpu.VMEM(shape, jnp.float32)],
+        compiler_params=PARAMS,
+    )(total)
+
+
+def split_kernel(bit, flips, *refs):
+    ways = 1 + len(flips)
     *addends, own_ref = refs[: len(refs) - ways + 1]
     send_refs = refs[len(refs) - ways + 1 :]
     count = own_ref.shape[0]
-    place = lax.axis_index("mpo")
-    digit = (place >> shift) & (ways - 1)
+    digit = (lax.axis_index("mpo") >> (1 + bit)) & (ways - 1)
 
     def summed(block):
         value = addends[0][block]
@@ -210,20 +251,19 @@
             value += other[block].astype(jnp.float32)
         return value
 
-    for ref, even, odd in zip(send_refs, *flips):
-        flip = jnp.where(place % 2 == 0, even, odd)
+    for ref, flip in zip(send_refs, flips):
         for at in range(count):
             ref[at] = summed((digit ^ flip) * count + at).astype(ref.dtype)
     for at in range(count):
         own_ref[at] = summed(digit * count + at)
 
 
-def split(addends, shift, flips):
-    ways = 1 + len(flips[0])
+def split(addends, bit, flips):
+    ways = 1 + len(flips)
     blocks, height, width = addends[0].shape
     shape = (blocks // ways, height, width)
     own, *sends = pl.pallas_call(
-        functools.partial(split_kernel, shift, flips),
+        functools.partial(split_kernel, bit, flips),
         in_specs=[VMEM] * len(addends),
         out_specs=[VMEM] * ways,
         out_shape=[pltpu.VMEM(shape, jnp.float32)] + [pltpu.VMEM(shape, jnp.bfloat16)] * (ways - 1),
@@ -234,11 +274,10 @@
 
 def local(psi, left_env, right_env, dims, term_shift, connect):
     sectors, group = lax.axis_size("sec"), lax.axis_size("mpo")
-    place = lax.axis_index("mpo")
     order = psi.shape[1]
 
     pieces = mask(dims, psi)
-    to_core = group_pairs(sectors, group, lambda core: 1)
+    to_core = group_pairs(sectors, group, 1)
     got = [lax.ppermute(piece, AXES, halo_pairs(sectors, group)) for piece in pieces]
     left, right, code, keep = load(sectors, group, dims, term_shift, connect, left_env, right_env)
     got[0], code = lax.optimization_barrier((got[0], code))
@@ -252,21 +291,15 @@
         sent = half(start, True, group, *last, *total)
         kept = half(start, False, group, *last, *total)
     else:
-        blocks = part(start, *last, total).reshape(group // 2, 2, order // group, order)
-        kept = lax.dynamic_index_in_dim(blocks, place % 2, 1, keepdims=False)
-        sent = lax.dynamic_index_in_dim(blocks, 1 - place % 2, 1, keepdims=False).astype(jnp.bfloat16)
+        sent, kept = pick(group, part(start, *last, total))
 
     addends = [kept, lax.ppermute(sent, AXES, to_core)]
-    bits = (group // 2).bit_length() - 1
-    while bits:
-        taken = min(bits, 2)
-        bits -= taken
-        flips = [(1, 2, 3), (2, 1, 3)] if taken == 2 else [(1,), (1,)]
-        sends, own = split(addends, 1 + bits, flips)
+    for bit, ways in stages_of(group):
+        flips = FLIPS[ways]
+        sends, own = split(addends, bit, flips)
         addends = [own]
-        for sent, even, odd in zip(sends, *flips):
-            partners = group_pairs(sectors, group, lambda core: (odd if core else even) << (1 + bits))
-            addends.append(lax.ppermute(sent, AXES, partners))
+        for sent, flip in zip(sends, flips):
+            addends.append(lax.ppermute(sent, AXES, group_pairs(sectors, group, (flip << (1 + bit)) | 1)))
     value = addends[0]
     for other in addends[1:]:
         value = value + other.astype(jnp.float32)

time: 25 us -> 22.9 us (0.916)
  waiting for transfers between devices: 10.7 us -> 9.06 us
  starting transfers between devices: 7.09 us -> 6.63 us
    ppermute x3, waiting for transfers between devices: 5.13 us -> 3.88 us  [local(): lax.ppermute(sent, AXES, group_pairs(sectors, group, flip << 1 + bit | 1))]
    ppermute x2, starting transfers between devices: 3.17 us -> 2.61 us  [local(): lax.ppermute(piece, AXES, halo_pairs(sectors, group))]
    ppermute x2, waiting for transfers between devices: 4.83 us -> 4.51 us  [local(): lax.ppermute(piece, AXES, halo_pairs(sectors, group))]
  transfers between devices with their start and end apart: 8 -> 8, of which waited for: 7 -> 7; matrix products, arithmetic and copies ran while one was open for 0% -> 0% of each run, Pallas kernels for 17% -> 19%
where the time goes in v4:
time: 22.9 us; the launch traced here: 22.8 us
  waiting for transfers between devices  9.06 us (40%)
  starting transfers between devices  6.63 us (29%)
  Pallas kernels  6.37 us (28%)
  other arithmetic  0.67 us (3%)
    ppermute x2, waiting for transfers between devices, local(): lax.ppermute(piece, AXES, halo_pairs(sectors, group))  4.51 us
    ppermute x3, waiting for transfers between devices, local(): lax.ppermute(sent, AXES, group_pairs(sectors, group, flip << 1 + bit | 1))  3.88 us
    ppermute x3, starting transfers between devices, local(): lax.ppermute(sent, AXES, group_pairs(sectors, group, flip << 1 + bit | 1))  3.6 us
    ppermute x2, starting transfers between devices, local(): lax.ppermute(piece, AXES, halo_pairs(sectors, group))  2.61 us
    pallas_call x1, Pallas kernels, load(): pl.pallas_call(functools.partial(load_kernel, sectors), in_specs=[HBM] *...  2.24 us
    pallas_call x2, Pallas kernels, half(): pl.pallas_call(functools.partial(half_kernel, start, theirs, group), in_s...  1.51 us
    pallas_call x1, Pallas kernels, part(): pl.pallas_call(functools.partial(part_kernel, start), in_specs=[VMEM] * l...  1.3 us
    pallas_call x1, Pallas kernels, mask(): pl.pallas_call(mask_kernel, in_specs=[HBM, HBM], out_specs=[VMEM] * len(C...  1.27 us
  transfers between devices with their start and end apart: 8, of which 7 were waited for; matrix products, arithmetic and copies ran while one was open for 0% of the time, Pallas kernels for 19%

profile of v4, /device:TPU:0, one launch (start us, length us, event | category | flops | bytes accessed | tf_op | source)
XLA Modules:
  0.0 22.8 jit_solution(5705558226316595613)
XLA Ops:
  0.0 1.3 %shard_map.65 = (bf16[512,256]{1,0:T(8,128)(2,1)S(1)}, bf16[512,256]{1,0:T(8,128)(2,1)S(1)}) custom-call(s32[1,2]{1,0:T(1,128)} %dims_hbm.3, bf16[1,512,512]{2,1,0:T(8,128)(2,1)} %psi_hbm.1), custom_call_target="tpu_custom_call" | custom-call | tf_op jit(solution)/shard_map/pallas_call | solution.py:85
  1.3 2.5 %collective-permute-start = (bf16[512,256]{1,0:T(8,128)(2,1)S(1)}, bf16[512,256]{1,0:T(8,128)(2,1)S(1)}, u32[]{:S(2)}, u32[]{:S(2)}) collective-permute-start(bf16[512,256]{1,0:T(8,128)(2,1)S(1)} %get-tuple-element.18.own_ref), channel_id=1, source_target_pairs={{0,9},{1,3},{2,11},{3,1},{4,13},{5,7},{6,15},{7,5},{8,17},{9,0},{1... | collective-permute-start | bytes 786440 | tf_op jit(solution)/shard_map/ppermute | solution.py:281
  3.8 0.1 collective-permute-start.1
  3.9 2.2 %shard_map.64 = (bf16[4,512,512]{2,1,0:T(8,128)(2,1)S(1)}, bf16[4,512,512]{2,1,0:T(8,128)(2,1)S(1)}, s32[8,128]{1,0:T(8,128)S(1)}, f32[64,512]{1,0:T(8,128)S(1)}) custom-call(s32[1,2]{1,0:T(1,128)} %dims_hbm.3, s32[4]{0:T(128)} %shift_hbm.1, s32[1,4]{1,0:T(1,128)} %connect_hbm.1, bf16[1,4,512,512]{3,2,1,0:T(8,128)(2,1)} %left_hbm.1, ...), custom_call_target="tpu_custom_call" | custom-call | flops 2147483648 | bytes 4194304 | tf_op jit(solution)/shard_map/pallas_call | solution.py:133
  6.1 1.7 %collective-permute-done.got_ref = bf16[512,256]{1,0:T(8,128)(2,1)S(1)} collective-permute-done((bf16[512,256]{1,0:T(8,128)(2,1)S(1)}, bf16[512,256]{1,0:T(8,128)(2,1)S(1)}, u32[]{:S(2)}, u32[]{:S(2)}) %collective-permute-start) | collective-permute-done | bytes 262176 | tf_op jit(solution)/shard_map/ppermute | solution.py:281
  7.9 0.0 collective-permute-start.3
  7.9 2.8 %collective-permute-done.1.got_ref = bf16[512,256]{1,0:T(8,128)(2,1)S(1)} collective-permute-done((bf16[512,256]{1,0:T(8,128)(2,1)S(1)}, bf16[512,256]{1,0:T(8,128)(2,1)S(1)}, u32[]{:S(2)}, u32[]{:S(2)}) %collective-permute-start.1) | collective-permute-done | bytes 262176 | tf_op jit(solution)/shard_map/ppermute | solution.py:281
  10.7 0.0 collective-permute-start.2
  10.7 0.0 collective-permute-done.3.swapped_ref
  10.7 1.3 %shard_map.66.before_ref = f32[512,512]{1,0:T(8,128)S(1)} custom-call(s32[8,128]{1,0:T(8,128)S(1)} %get-tuple-element.20.code_ref, bf16[512,256]{1,0:T(8,128)(2,1)S(1)} %get-tuple-element.18.own_ref, bf16[512,256]{1,0:T(8,128)(2,1)S(1)} %collective-permute-done.got_ref, bf16[512,256]{1,0:T(8,128)(2,1)S(1)} %collective-permute-done.3.swapped_ref, ...), custom_call_target="tpu_custom_call" | custom-call | tf_op jit(solution)/shard_map/pallas_call | solution.py:178
  12.0 0.2 collective-permute-done.2.swapped_ref
  12.2 0.8 %shard_map.68 = bf16[4,64,512]{2,1,0:T(8,128)(2,1)S(1)} custom-call(s32[8,128]{1,0:T(8,128)S(1)} %get-tuple-element.20.code_ref, bf16[512,256]{1,0:T(8,128)(2,1)S(1)} %get-tuple-element.21.own_ref, bf16[512,256]{1,0:T(8,128)(2,1)S(1)} %collective-permute-done.1.got_ref, bf16[512,256]{1,0:T(8,128)(2,1)S(1)} %collective-permute-done.2.swapped_ref, ...), custom_call_target="tpu_custom_call" | custom-call | flops 536870912 | tf_op jit(solution)/shard_map/pallas_call | solution.py:212
  13.0 0.4 %collective-permute-start.4 = (bf16[4,64,512]{2,1,0:T(8,128)(2,1)S(1)}, bf16[4,64,512]{2,1,0:T(8,128)(2,1)S(1)}, u32[]{:S(2)}, u32[]{:S(2)}) collective-permute-start(bf16[4,64,512]{2,1,0:T(8,128)(2,1)S(1)} %shard_map.68), channel_id=1, source_target_pairs={{0,1},{1,0},{2,3},{3,2},{4,5},{5,4},{6,7},{7,6},{8,9},{9,8},{10,11... | collective-permute-start | bytes 786440 | tf_op jit(solution)/shard_map/ppermute | solution.py:296
  13.3 0.8 %shard_map.67.refs_0_ = f32[4,64,512]{2,1,0:T(8,128)S(1)} custom-call(s32[8,128]{1,0:T(8,128)S(1)} %get-tuple-element.20.code_ref, bf16[512,256]{1,0:T(8,128)(2,1)S(1)} %get-tuple-element.21.own_ref, bf16[512,256]{1,0:T(8,128)(2,1)S(1)} %collective-permute-done.1.got_ref, bf16[512,256]{1,0:T(8,128)(2,1)S(1)} %collective-permute-done.2.swapped_ref, ...), custom_call_target="tpu_custom_call" | custom-call | flops 536870912 | tf_op jit(solution)/shard_map/pallas_call | solution.py:212
  14.1 0.5 %collective-permute-done.4.refs_1_ = bf16[4,64,512]{2,1,0:T(8,128)(2,1)S(1)} collective-permute-done((bf16[4,64,512]{2,1,0:T(8,128)(2,1)S(1)}, bf16[4,64,512]{2,1,0:T(8,128)(2,1)S(1)}, u32[]{:S(2)}, u32[]{:S(2)}) %collective-permute-start.4) | collective-permute-done | bytes 262176 | tf_op jit(solution)/shard_map/ppermute | solution.py:296
  14.6 3.1 %collective-permute-start.5 = (bf16[1,64,512]{2,1,0:T(8,128)(2,1)S(1)}, bf16[1,64,512]{2,1,0:T(8,128)(2,1)S(1)}, u32[]{:S(2)}, u32[]{:S(2)}) collective-permute-start(bf16[1,64,512]{2,1,0:T(8,128)(2,1)S(1)} %get-tuple-element.26), channel_id=1, source_target_pairs={{0,7},{1,6},{2,5},{3,4},{4,3},{5,2},{6,1},{7,0},{8,15},{9,14},{10,... | collective-permute-start | bytes 196616 | tf_op jit(solution)/shard_map/ppermute | solution.py:302
  17.8 0.4 %collective-permute-start.6 = (bf16[1,64,512]{2,1,0:T(8,128)(2,1)S(1)}, bf16[1,64,512]{2,1,0:T(8,128)(2,1)S(1)}, u32[]{:S(2)}, u32[]{:S(2)}) collective-permute-start(bf16[1,64,512]{2,1,0:T(8,128)(2,1)S(1)} %get-tuple-element.27), channel_id=1, source_target_pairs={{0,3},{1,2},{2,1},{3,0},{4,7},{5,6},{6,5},{7,4},{8,11},{9,10},{10,... | collective-permute-start | bytes 196616 | tf_op jit(solution)/shard_map/ppermute | solution.py:302
  18.1 0.1 collective-permute-start.7
  18.2 1.9 %collective-permute-done.5 = bf16[1,64,512]{2,1,0:T(8,128)(2,1)S(1)} collective-permute-done((bf16[1,64,512]{2,1,0:T(8,128)(2,1)S(1)}, bf16[1,64,512]{2,1,0:T(8,128)(2,1)S(1)}, u32[]{:S(2)}, u32[]{:S(2)}) %collective-permute-start.5) | collective-permute-done | bytes 65568 | tf_op jit(solution)/shard_map/ppermute | solution.py:302
  20.2 1.7 %collective-permute-done.6 = bf16[1,64,512]{2,1,0:T(8,128)(2,1)S(1)} collective-permute-done((bf16[1,64,512]{2,1,0:T(8,128)(2,1)S(1)}, bf16[1,64,512]{2,1,0:T(8,128)(2,1)S(1)}, u32[]{:S(2)}, u32[]{:S(2)}) %collective-permute-start.6) | collective-permute-done | bytes 65568 | tf_op jit(solution)/shard_map/ppermute | solution.py:302
  21.9 0.2 %collective-permute-done.7 = bf16[1,64,512]{2,1,0:T(8,128)(2,1)S(1)} collective-permute-done((bf16[1,64,512]{2,1,0:T(8,128)(2,1)S(1)}, bf16[1,64,512]{2,1,0:T(8,128)(2,1)S(1)}, u32[]{:S(2)}, u32[]{:S(2)}) %collective-permute-start.7) | collective-permute-done | bytes 65568 | tf_op jit(solution)/shard_map/ppermute | solution.py:302
  22.1 0.7 %fusion.1 = bf16[1,64,512]{2,1,0:T(8,128)(2,1)} fusion(bf16[1,64,512]{2,1,0:T(8,128)(2,1)S(1)} %collective-permute-done.7, bf16[1,64,512]{2,1,0:T(8,128)(2,1)S(1)} %collective-permute-done.6, f32[1,64,512]{2,1,0:T(8,128)S(1)} %get-tuple-element.25, bf16[1,64,512]{2,1,0:T(8,128)(2,1)S(1)} %collective-permute-done.5, f32[64,512]{1,0:T(8,128)S(1)} %get-tuple-element.17), kind=kLoop, calls=%fused_computation.2 | loop fusion | flops 294912 | bytes 524288 | tf_op jit(solution)/shard_map/broadcast_in_dim | solution.py:307
  (1 shorter events, 0.0 us)
Async XLA Ops:
  1.3 6.6 %collective-permute-start = (bf16[512,256]{1,0:T(8,128)(2,1)S(1)}, bf16[512,256]{1,0:T(8,128)(2,1)S(1)}, u32[]{:S(2)}, u32[]{:S(2)}) collective-permute-start(bf16[512,256]{1,0:T(8,128)(2,1)S(1)} %get-tuple-element.18.own_ref), channel_id=1, source_target_pairs={{0,9},{1,3},{2,11},{3,1},{4,13},{5,7},{6,15},{7,5},{8,17},{9,0},{1... | collective-permute-start | bytes 786440 | tf_op jit(solution)/shard_map/ppermute | solution.py:281
  3.8 6.9 %collective-permute-start.1 = (bf16[512,256]{1,0:T(8,128)(2,1)S(1)}, bf16[512,256]{1,0:T(8,128)(2,1)S(1)}, u32[]{:S(2)}, u32[]{:S(2)}) collective-permute-start(bf16[512,256]{1,0:T(8,128)(2,1)S(1)} %get-tuple-element.21.own_ref), channel_id=1, source_target_pairs={{0,9},{1,3},{2,11},{3,1},{4,13},{5,7},{6,15},{7,5},{8,17},{9,0},{1... | collective-permute-start | bytes 786440 | tf_op jit(solution)/shard_map/ppermute | solution.py:281
  7.9 2.8 %collective-permute-start.3 = (bf16[512,256]{1,0:T(8,128)(2,1)S(1)}, bf16[512,256]{1,0:T(8,128)(2,1)S(1)}, u32[]{:S(2)}, u32[]{:S(2)}) collective-permute-start(bf16[512,256]{1,0:T(8,128)(2,1)S(1)} %collective-permute-done.got_ref), channel_id=1, source_target_pairs={{0,1},{1,0},{2,3},{3,2},{4,5},{5,4},{6,7},{7,6},{8,9},{9,8},{10,11... | collective-permute-start | bytes 786440 | tf_op jit(solution)/shard_map/ppermute | solution.py:284
  10.7 1.5 %collective-permute-start.2 = (bf16[512,256]{1,0:T(8,128)(2,1)S(1)}, bf16[512,256]{1,0:T(8,128)(2,1)S(1)}, u32[]{:S(2)}, u32[]{:S(2)}) collective-permute-start(bf16[512,256]{1,0:T(8,128)(2,1)S(1)} %collective-permute-done.1.got_ref), channel_id=1, source_target_pairs={{0,1},{1,0},{2,3},{3,2},{4,5},{5,4},{6,7},{7,6},{8,9},{9,8},{10,11... | collective-permute-start | bytes 786440 | tf_op jit(solution)/shard_map/ppermute | solution.py:284
  13.0 1.6 %collective-permute-start.4 = (bf16[4,64,512]{2,1,0:T(8,128)(2,1)S(1)}, bf16[4,64,512]{2,1,0:T(8,128)(2,1)S(1)}, u32[]{:S(2)}, u32[]{:S(2)}) collective-permute-start(bf16[4,64,512]{2,1,0:T(8,128)(2,1)S(1)} %shard_map.68), channel_id=1, source_target_pairs={{0,1},{1,0},{2,3},{3,2},{4,5},{5,4},{6,7},{7,6},{8,9},{9,8},{10,11... | collective-permute-start | bytes 786440 | tf_op jit(solution)/shard_map/ppermute | solution.py:296
  14.6 5.5 %collective-permute-start.5 = (bf16[1,64,512]{2,1,0:T(8,128)(2,1)S(1)}, bf16[1,64,512]{2,1,0:T(8,128)(2,1)S(1)}, u32[]{:S(2)}, u32[]{:S(2)}) collective-permute-start(bf16[1,64,512]{2,1,0:T(8,128)(2,1)S(1)} %get-tuple-element.26), channel_id=1, source_target_pairs={{0,7},{1,6},{2,5},{3,4},{4,3},{5,2},{6,1},{7,0},{8,15},{9,14},{10,... | collective-permute-start | bytes 196616 | tf_op jit(solution)/shard_map/ppermute | solution.py:302
  17.8 4.1 %collective-permute-start.6 = (bf16[1,64,512]{2,1,0:T(8,128)(2,1)S(1)}, bf16[1,64,512]{2,1,0:T(8,128)(2,1)S(1)}, u32[]{:S(2)}, u32[]{:S(2)}) collective-permute-start(bf16[1,64,512]{2,1,0:T(8,128)(2,1)S(1)} %get-tuple-element.27), channel_id=1, source_target_pairs={{0,3},{1,2},{2,1},{3,0},{4,7},{5,6},{6,5},{7,4},{8,11},{9,10},{10,... | collective-permute-start | bytes 196616 | tf_op jit(solution)/shard_map/ppermute | solution.py:302
  18.1 4.0 %collective-permute-start.7 = (bf16[1,64,512]{2,1,0:T(8,128)(2,1)S(1)}, bf16[1,64,512]{2,1,0:T(8,128)(2,1)S(1)}, u32[]{:S(2)}, u32[]{:S(2)}) collective-permute-start(bf16[1,64,512]{2,1,0:T(8,128)(2,1)S(1)} %get-tuple-element.28), channel_id=1, source_target_pairs={{0,5},{1,4},{2,7},{3,6},{4,1},{5,0},{6,3},{7,2},{8,13},{9,12},{10,... | collective-permute-start | bytes 196616 | tf_op jit(solution)/shard_map/ppermute | solution.py:302

commit v5 on v4

v5 whole, which is shorter than its diff:
```python
import functools

import jax
import jax.numpy as jnp
from jax import lax
from jax.experimental import pallas as pl
from jax.experimental.pallas import tpu as pltpu
from jax.sharding import PartitionSpec as P

AXES = ("sec", "mpo")
CUTS = (256, 256)
FLIPS = {4: (3, 1, 2), 2: (1,), 1: ()}
VMEM = pl.BlockSpec(memory_space=pltpu.VMEM)
HBM = pl.BlockSpec(memory_space=pltpu.HBM)
PARAMS = pltpu.CompilerParams(vmem_limit_bytes=8 * 1024 * 1024)


def halo_pairs(sectors, group):
    pairs = []
    for sector in range(sectors):
        for place in range(group):
            there = sector + 1 if place % 2 == 0 else sector - 1
            if 0 <= there < sectors:
                pairs.append((sector * group + place, there * group + (place ^ 1)))
            elif group % 4 == 0:
                pairs.append((sector * group + place, sector * group + (place ^ 2)))
    return pairs


def group_pairs(sectors, group, flip):
    return [
        (sector * group + place, sector * group + (place ^ flip))
        for sector in range(sectors)
        for place in range(group)
    ]


def stages_of(group):
    bits, stages = (group // 2).bit_length() - 1, []
    while bits:
        taken = min(bits, 2)
        bits -= taken
        stages.append((bits, 1 << taken))
    return stages or [(0, 1)]


def parity(number):
    for shift in (8, 4, 2, 1):
        number = number ^ (number >> shift)
    return number & 1


def in_hbm(array):
    return pltpu.with_memory_space_constraint(array, pltpu.HBM)


def dot(a, b):
    return jnp.dot(a, b, preferred_element_type=jnp.float32)


def mask_kernel(start, dims_hbm, psi_hbm, out_ref, dims_ref, psi_ref, sems):
    parts = sems.shape[0] - 1
    rows, width = out_ref.shape[0] // parts, out_ref.shape[1]
    dims_copy = pltpu.make_async_copy(dims_hbm, dims_ref, sems.at[parts])
    dims_copy.start()
    copies = []
    for at in range(parts):
        from_ref = psi_hbm.at[0, pl.ds(at * rows, rows), pl.ds(start, width)]
        copies.append(pltpu.make_async_copy(from_ref, psi_ref.at[pl.ds(at * rows, rows)], sems.at[at]))
        copies[-1].start()
    dims_copy.wait()
    for at in range(parts):
        row = lax.broadcasted_iota(jnp.int32, (rows, width), 0) + at * rows
        col = lax.broadcasted_iota(jnp.int32, (rows, width), 1) + start
        keep = (row < dims_ref[0, 0] * 32) & (col < dims_ref[0, 1] * 32)
        copies[at].wait()
        piece = psi_ref[pl.ds(at * rows, rows)]
        out_ref[pl.ds(at * rows, rows)] = jnp.where(keep, piece, jnp.zeros_like(piece))


def mask(start, width, dims, psi):
    order, parts = psi.shape[1], 8
    return pl.pallas_call(
        functools.partial(mask_kernel, start),
        in_specs=[HBM, HBM],
        out_specs=VMEM,
        out_shape=pltpu.VMEM((order, width), psi.dtype),
        scratch_shapes=[
            pltpu.SMEM(dims.shape, jnp.int32),
            pltpu.VMEM((order, width), psi.dtype),
            pltpu.SemaphoreType.DMA((parts + 1,)),
        ],
        compiler_params=PARAMS,
        cost_estimate=pl.CostEstimate(flops=50000000000 if start else 0, bytes_accessed=0, transcendentals=0),
    )(in_hbm(dims), in_hbm(psi))


def load_kernel(sectors, dims_hbm, shift_hbm, connect_hbm, left_hbm, right_hbm, left_ref, right_ref, code_ref, keep_ref, dims_ref, shift_ref, connect_ref, sems):
    terms = left_ref.shape[0]
    scalars = [(dims_hbm, dims_ref), (shift_hbm, shift_ref), (connect_hbm, connect_ref)]
    copies = [pltpu.make_async_copy(a, b, sems.at[at]) for at, (a, b) in enumerate(scalars)]
    for term in range(terms):
        for which, (a, b) in enumerate(((left_hbm, left_ref), (right_hbm, right_ref))):
            copies.append(pltpu.make_async_copy(a.at[0, term], b.at[term], sems.at[len(copies)]))
    for copy in copies:
        copy.start()
    for copy in copies[:3]:
        copy.wait()

    sector, place = lax.axis_index("sec"), lax.axis_index("mpo")
    above = place % 2 == 0
    code = jnp.int32(0)
    for term in range(terms):
        shift = shift_ref[term]
        there = sector - shift
        used = (connect_ref[0, term] != 0) & (there >= 0) & (there < sectors)
        direct = (shift < 0) == above
        choice = jnp.where(shift == 0, 3, jnp.where(direct, 2, 1))
        code += jnp.where(used, choice, 0) << (2 * term)
    code_ref[...] = jnp.full(code_ref.shape, code, jnp.int32)

    rows = lax.broadcasted_iota(jnp.int32, keep_ref.shape, 0) + place * keep_ref.shape[0]
    cols = lax.broadcasted_iota(jnp.int32, keep_ref.shape, 1)
    keep = (rows < dims_ref[0, 0] * 32) & (cols < dims_ref[0, 1] * 32)
    keep_ref[...] = jnp.where(keep, 1.0, 0.0)
    for copy in copies[3:]:
        copy.wait()


def load(sectors, group, dims, term_shift, connect, left, right):
    _, terms, order, _ = left.shape
    return pl.pallas_call(
        functools.partial(load_kernel, sectors),
        in_specs=[HBM] * 5,
        out_specs=[VMEM] * 4,
        out_shape=[
            pltpu.VMEM(left.shape[1:], left.dtype),
            pltpu.VMEM(right.shape[1:], right.dtype),
            pltpu.VMEM((8, 128), jnp.int32),
            pltpu.VMEM((order // group, order), jnp.float32),
        ],
        scratch_shapes=[
            pltpu.SMEM(dims.shape, jnp.int32),
            pltpu.SMEM(term_shift.shape, jnp.int32),
            pltpu.SMEM(connect.shape, jnp.int32),
            pltpu.SemaphoreType.DMA((2 * terms + 3,)),
        ],
        compiler_params=PARAMS,
        cost_estimate=pl.CostEstimate(flops=4 * terms * order**3, bytes_accessed=4 * terms * order**2, transcendentals=0),
    )(*[in_hbm(array) for array in (dims, term_shift, connect, left, right)])


def row_blocks(group, height, flips):
    place = lax.axis_index("mpo")
    bit, ways = stages_of(group)[0]
    digit = (place >> (1 + bit)) & (ways - 1)
    firsts = []
    for flip in (0, *flips):
        for at in range(1 << bit):
            chip = ((digit ^ flip) << bit) + at
            firsts.append((2 * chip + (parity(place) ^ parity(chip))) * height)
    return [pl.ds(pl.multiple_of(first, height), height) for first in firsts]


def products(start, places, sources, groups, first_ref):
    own, got, swapped = (ref[...] for ref in sources)
    total = None
    for code_ref, left_ref, right_ref, direct in groups:
        code = code_ref[0, 0]
        terms, order, _ = right_ref.shape
        width = own.shape[1]
        for term in range(terms):
            choice = (code >> (2 * term)) & 3
            source = jnp.where(choice == direct, got, jnp.where(choice == 3 - direct, swapped, jnp.zeros_like(own)))
            source = jnp.where(choice == 3, own, source)
            left = left_ref[term] if places is None else jnp.concatenate([left_ref[term, at] for at in places], axis=0)
            first_ref[:, term * width : (term + 1) * width] = dot(left, source).astype(jnp.bfloat16)
        right = right_ref[:, start : start + width, :].reshape(terms * width, order)
        total = dot(first_ref[...], right) if total is None else total + dot(first_ref[...], right)
    return total


def sums_kernel(start, group, height, flips, last, *refs):
    sources, (code, left, right, code_2, left_2, right_2), refs = refs[:3], refs[3:9], refs[9:]
    order = left.shape[1]
    groups = ((code, left, right, 2), (code_2, left_2.at[0], right_2.at[0], 1))
    places = row_blocks(group, height, flips)
    narrow = height % 16 == 0
    *before, first_ref, total_ref = refs[: -(2 + (1 + len(flips) if last else 1))] + refs[-2:]
    outs = refs[len(before) : -2]
    total = products(start, places if narrow else None, sources, groups, first_ref)
    for ref in before:
        total += ref[...]
    if not last:
        outs[0][...] = total
        return
    if not narrow:
        total_ref[...] = total
    each = len(places) // len(outs)
    for which, out_ref in enumerate(outs):
        for at in range(each):
            block = which * each + at
            value = total[block * height : (block + 1) * height] if narrow else total_ref[places[block]]
            out_ref[at] = value.astype(out_ref.dtype)


def sums(start, group, flips, last, sources, terms, before):
    count, order, _ = terms[1].shape
    height = order // group
    rows = order // 2 if height % 16 == 0 else order
    shape = (group // 2 // (1 + len(flips)), height, order)
    if last:
        outs = [pltpu.VMEM(shape, jnp.float32)] + [pltpu.VMEM(shape, jnp.bfloat16)] * len(flips)
    else:
        outs = [pltpu.VMEM((rows, order), jnp.float32)]
    operands = [*sources, *terms, *before]
    return pl.pallas_call(
        functools.partial(sums_kernel, start, group, height, flips, last),
        in_specs=[VMEM] * len(operands),
        out_specs=[VMEM] * len(outs),
        out_shape=outs,
        scratch_shapes=[
            pltpu.VMEM((rows, count * sources[0].shape[1]), jnp.bfloat16),
            pltpu.VMEM((order, order) if height % 16 else (8, 128), jnp.float32),
        ],
        compiler_params=PARAMS,
    )(*operands)


def split_kernel(bit, flips, *refs):
    ways = 1 + len(flips)
    *addends, own_ref = refs[: len(refs) - ways + 1]
    send_refs = refs[len(refs) - ways + 1 :]
    count = own_ref.shape[0]
    digit = (lax.axis_index("mpo") >> (1 + bit)) & (ways - 1)

    def summed(block):
        value = addends[0][block]
        for other in addends[1:]:
            value += other[block].astype(jnp.float32)
        return value

    for ref, flip in zip(send_refs, flips):
        for at in range(count):
            ref[at] = summed((digit ^ flip) * count + at).astype(ref.dtype)
    for at in range(count):
        own_ref[at] = summed(digit * count + at)


def split(addends, bit, flips):
    ways = 1 + len(flips)
    blocks, height, width = addends[0].shape
    shape = (blocks // ways, height, width)
    own, *sends = pl.pallas_call(
        functools.partial(split_kernel, bit, flips),
        in_specs=[VMEM] * len(addends),
        out_specs=[VMEM] * ways,
        out_shape=[pltpu.VMEM(shape, jnp.float32)] + [pltpu.VMEM(shape, jnp.bfloat16)] * (ways - 1),
        compiler_params=PARAMS,
    )(*addends)
    return sends, own


def local(psi, left_env, right_env, dims, term_shift, connect):
    sectors, group = lax.axis_size("sec"), lax.axis_size("mpo")
    order = psi.shape[1]

    pieces, start = [], 0
    for cut in CUTS:
        pieces.append(mask(start, cut, dims, psi))
        pieces[-1], psi = lax.optimization_barrier((pieces[-1], psi))
        start += cut
    to_core = group_pairs(sectors, group, 1)
    got = [lax.ppermute(piece, AXES, halo_pairs(sectors, group)) for piece in pieces]
    left_env, right_env, pieces[0] = lax.optimization_barrier((left_env, right_env, pieces[0]))
    left_2, right_2 = (lax.ppermute(env, AXES, to_core) for env in (left_env, right_env))
    left, right, code, keep = load(sectors, group, dims, term_shift, connect, left_env, right_env)
    code_2 = lax.ppermute(code, AXES, to_core)
    got[0], code = lax.optimization_barrier((got[0], code))
    got[-1], code_2 = lax.optimization_barrier((got[-1], code_2))
    swapped = [lax.ppermute(piece, AXES, to_core) for piece in got]

    terms = (code, left, right, code_2, left_2, right_2)
    stages = stages_of(group)
    start, addends = 0, []
    for at, cut in enumerate(CUTS):
        last = at == len(CUTS) - 1
        addends = sums(start, group, FLIPS[stages[0][1]], last, (pieces[at], got[at], swapped[at]), terms, addends)
        start += cut
    own, *sends = addends
    for at, (bit, ways) in enumerate(stages):
        if at > 0:
            sends, own = split(addends, bit, FLIPS[ways])
        addends = [own]
        for sent, flip in zip(sends, FLIPS[ways]):
            addends.append(lax.ppermute(sent, AXES, group_pairs(sectors, group, (flip << (1 + bit)) | parity(flip))))
    value = addends[0]
    for other in addends[1:]:
        value = value + other.astype(jnp.float32)
    value = jnp.where(keep != 0, value.reshape(keep.shape), 0.0)
    return value.astype(jnp.bfloat16)[None]


def solution(mesh):
    placed = (
        P("sec", None, None),
        P("sec", "mpo", None, None),
        P("sec", "mpo", None, None),
        P("sec", None),
        P("mpo"),
        P("sec", "mpo"),
    )
    return jax.shard_map(
        local, mesh=mesh, in_specs=placed, out_specs=P("sec", "mpo", None), check_vma=False
    )
```

time: 22.9 us -> 21.6 us (0.943)
  waiting for transfers between devices: 9.06 us -> 5.64 us
  starting transfers between devices: 6.63 us -> 8.14 us
  Pallas kernels: 6.37 us -> 6.8 us
    ppermute x2, waiting for transfers between devices: 4.51 us -> 0.17 us  [local(): lax.ppermute(piece, AXES, halo_pairs(sectors, group))]
    ppermute x2, starting transfers between devices: 2.61 us -> 3.78 us  [local(): lax.ppermute(piece, AXES, halo_pairs(sectors, group))]
    ppermute x4 -> x6, waiting for transfers between devices: 4.35 us -> 5.26 us  [the longest x3 3.65 us: local(): lax.ppermute(sent, AXES, group_pairs(sectors, group, flip << 1 + bit | pa...]
    pallas_call x5 -> x4, Pallas kernels: 4.13 us -> 4.56 us  [the longest x2 2.64 us: sums(): pl.pallas_call(functools.partial(sums_kernel, start, group, height, flips...]
    ppermute x2, starting transfers between devices: 0.06 us -> 0.48 us  [local(): swapped = [lax.ppermute(piece, AXES, to_core) for piece in got]]
    ppermute x4 -> x6, starting transfers between devices: 3.96 us -> 3.88 us  [the longest x3 3.27 us: local(): lax.ppermute(sent, AXES, group_pairs(sectors, group, flip << 1 + bit | pa...]
  transfers between devices with their start and end apart: 8 -> 10, of which waited for: 7 -> 5; matrix products, arithmetic and copies ran while one was open for 0% -> 0% of each run, Pallas kernels for 19% -> 21%
where the time goes in v5:
time: 21.6 us; the launch traced here: 21.3 us
  starting transfers between devices  8.14 us (38%)
  Pallas kernels  6.8 us (31%)
  waiting for transfers between devices  5.64 us (26%)
  other arithmetic  0.68 us (3%)
    ppermute x2, starting transfers between devices, local(): lax.ppermute(piece, AXES, halo_pairs(sectors, group))  3.78 us
    ppermute x3, waiting for transfers between devices, local(): lax.ppermute(sent, AXES, group_pairs(sectors, group, flip << 1 + bit | pa...  3.65 us
    ppermute x3, starting transfers between devices, local(): lax.ppermute(sent, AXES, group_pairs(sectors, group, flip << 1 + bit | pa...  3.27 us
    pallas_call x2, Pallas kernels, sums(): pl.pallas_call(functools.partial(sums_kernel, start, group, height, flips...  2.64 us
    pallas_call x1, Pallas kernels, load(): pl.pallas_call(functools.partial(load_kernel, sectors), in_specs=[HBM] *...  2.24 us
    pallas_call x2, Pallas kernels, mask(): pl.pallas_call(functools.partial(mask_kernel, start), in_specs=[HBM, HBM]...  1.91 us
    ppermute x1, waiting for transfers between devices, local(): code_2 = lax.ppermute(code, AXES, to_core)  1.61 us
    broadcast_in_dim x1, other arithmetic, local(): return value.astype(jnp.bfloat16)[None]  0.68 us
  transfers between devices with their start and end apart: 10, of which 5 were waited for; matrix products, arithmetic and copies ran while one was open for 0% of the time, Pallas kernels for 21%

profile of v5, /device:TPU:0, one launch (start us, length us, event | category | flops | bytes accessed | tf_op | source)
XLA Modules:
  0.0 21.3 jit_solution(842235419161326145)
XLA Ops:
  0.0 1.0 %shard_map.64.refs_0_ = bf16[512,256]{1,0:T(8,128)(2,1)S(1)} custom-call(s32[1,2]{1,0:T(1,128)} %dims_hbm.5, bf16[1,512,512]{2,1,0:T(8,128)(2,1)} %psi_hbm.2), custom_call_target="tpu_custom_call" | custom-call | tf_op jit(solution)/shard_map/pallas_call | solution.py:83
  1.0 2.5 %collective-permute-start.3 = (bf16[512,256]{1,0:T(8,128)(2,1)S(1)}, bf16[512,256]{1,0:T(8,128)(2,1)S(1)}, u32[]{:S(2)}, u32[]{:S(2)}) collective-permute-start(bf16[512,256]{1,0:T(8,128)(2,1)S(1)} %shard_map.64.refs_0_), channel_id=1, source_target_pairs={{0,9},{1,3},{2,11},{3,1},{4,13},{5,7},{6,15},{7,5},{8,17},{9,0},{1... | collective-permute-start | bytes 786440 | tf_op jit(solution)/shard_map/ppermute | solution.py:274
  3.5 0.0 collective-permute-start.4
  3.5 0.5 %collective-permute-start.5 = (bf16[1,4,512,512]{3,2,1,0:T(8,128)(2,1)}, bf16[1,4,512,512]{3,2,1,0:T(8,128)(2,1)S(1)}, u32[]{:S(2)}, u32[]{:S(2)}) collective-permute-start(bf16[1,4,512,512]{3,2,1,0:T(8,128)(2,1)} %right_hbm), channel_id=1, source_target_pairs={{0,1},{1,0},{2,3},{3,2},{4,5},{5,4},{6,7},{7,6},{8,9},{9,8},{10,11... | collective-permute-start | bytes 6291464 | tf_op jit(solution)/shard_map/ppermute | solution.py:276
  4.0 1.0 %shard_map.66.refs_0_ = bf16[512,256]{1,0:T(8,128)(2,1)S(1)} custom-call(s32[1,2]{1,0:T(1,128)} %dims_hbm.5, bf16[1,512,512]{2,1,0:T(8,128)(2,1)} %psi_hbm.2), custom_call_target="tpu_custom_call" | custom-call | flops 49999998976 | tf_op jit(solution)/shard_map/pallas_call | solution.py:83
  5.0 1.2 %collective-permute-start = (bf16[512,256]{1,0:T(8,128)(2,1)S(1)}, bf16[512,256]{1,0:T(8,128)(2,1)S(1)}, u32[]{:S(2)}, u32[]{:S(2)}) collective-permute-start(bf16[512,256]{1,0:T(8,128)(2,1)S(1)} %shard_map.66.refs_0_), channel_id=1, source_target_pairs={{0,9},{1,3},{2,11},{3,1},{4,13},{5,7},{6,15},{7,5},{8,17},{9,0},{1... | collective-permute-start | bytes 786440 | tf_op jit(solution)/shard_map/ppermute | solution.py:274
  6.2 2.2 %shard_map.65 = (bf16[4,512,512]{2,1,0:T(8,128)(2,1)S(1)}, bf16[4,512,512]{2,1,0:T(8,128)(2,1)S(1)}, s32[8,128]{1,0:T(8,128)S(1)}, f32[64,512]{1,0:T(8,128)S(1)}) custom-call(s32[1,2]{1,0:T(1,128)} %dims_hbm.5, s32[4]{0:T(128)} %shift_hbm.1, s32[1,4]{1,0:T(1,128)} %connect_hbm.1, bf16[1,4,512,512]{3,2,1,0:T(8,128)(2,1)} %left_hbm, ...), custom_call_target="tpu_custom_call" | custom-call | flops 2147483648 | bytes 4194304 | tf_op jit(solution)/shard_map/pallas_call | solution.py:132
  8.5 0.1 collective-permute-start.1
  8.6 0.0 collective-permute-done.3.refs_1_
  8.6 0.5 %collective-permute-start.6 = (bf16[512,256]{1,0:T(8,128)(2,1)S(1)}, bf16[512,256]{1,0:T(8,128)(2,1)S(1)}, u32[]{:S(2)}, u32[]{:S(2)}) collective-permute-start(bf16[512,256]{1,0:T(8,128)(2,1)S(1)} %collective-permute-done.3.refs_1_), channel_id=1, source_target_pairs={{0,1},{1,0},{2,3},{3,2},{4,5},{5,4},{6,7},{7,6},{8,9},{9,8},{10,11... | collective-permute-start | bytes 786440 | tf_op jit(solution)/shard_map/ppermute | solution.py:281
  9.0 1.6 %collective-permute-done.1.refs_6_ = s32[8,128]{1,0:T(8,128)S(1)} collective-permute-done((s32[8,128]{1,0:T(8,128)S(1)}, s32[8,128]{1,0:T(8,128)S(1)}, u32[]{:S(2)}, u32[]{:S(2)}) %collective-permute-start.1) | collective-permute-done | bytes 4128 | tf_op jit(solution)/shard_map/ppermute | solution.py:278
  10.7 0.2 collective-permute-done.refs_1_
  10.8 0.0 collective-permute-start.2
  10.8 0.2 collective-permute-done.6.refs_2_
  11.0 0.0 collective-permute-done.4.refs_7_
  11.0 0.0 collective-permute-done.5.refs_8_
  11.0 1.3 %shard_map.67.refs_9_ = f32[256,512]{1,0:T(8,128)S(1)} custom-call(bf16[512,256]{1,0:T(8,128)(2,1)S(1)} %shard_map.64.refs_0_, bf16[512,256]{1,0:T(8,128)(2,1)S(1)} %collective-permute-done.3.refs_1_, bf16[512,256]{1,0:T(8,128)(2,1)S(1)} %collective-permute-done.6.refs_2_, s32[8,128]{1,0:T(8,128)S(1)} %get-tuple-element.31.refs_3_, ...), custom_call_target="tpu_custom_call" | custom-call | tf_op jit(solution)/shard_map/pallas_call | solution.py:217
  12.4 0.0 collective-permute-done.2.refs_2_
  12.4 1.3 %shard_map.68 = (f32[1,64,512]{2,1,0:T(8,128)S(1)}, bf16[1,64,512]{2,1,0:T(8,128)(2,1)S(1)}, bf16[1,64,512]{2,1,0:T(8,128)(2,1)S(1)}, bf16[1,64,512]{2,1,0:T(8,128)(2,1)S(1)}) custom-call(bf16[512,256]{1,0:T(8,128)(2,1)S(1)} %shard_map.66.refs_0_, bf16[512,256]{1,0:T(8,128)(2,1)S(1)} %collective-permute-done.refs_1_, ...), custom_call_target="tpu_custom_call" | custom-call | tf_op jit(solution)/shard_map/pallas_call | solution.py:217
  13.7 2.8 %collective-permute-start.7 = (bf16[1,64,512]{2,1,0:T(8,128)(2,1)S(1)}, bf16[1,64,512]{2,1,0:T(8,128)(2,1)S(1)}, u32[]{:S(2)}, u32[]{:S(2)}) collective-permute-start(bf16[1,64,512]{2,1,0:T(8,128)(2,1)S(1)} %get-tuple-element.38), channel_id=1, source_target_pairs={{0,6},{1,7},{2,4},{3,5},{4,2},{5,3},{6,0},{7,1},{8,14},{9,15},{10,... | collective-permute-start | bytes 196616 | tf_op jit(solution)/shard_map/ppermute | solution.py:296
  16.5 0.2 collective-permute-start.8
  16.7 0.3 %collective-permute-start.9 = (bf16[1,64,512]{2,1,0:T(8,128)(2,1)S(1)}, bf16[1,64,512]{2,1,0:T(8,128)(2,1)S(1)}, u32[]{:S(2)}, u32[]{:S(2)}) collective-permute-start(bf16[1,64,512]{2,1,0:T(8,128)(2,1)S(1)} %get-tuple-element.40), channel_id=1, source_target_pairs={{0,5},{1,4},{2,7},{3,6},{4,1},{5,0},{6,3},{7,2},{8,13},{9,12},{10,... | collective-permute-start | bytes 196616 | tf_op jit(solution)/shard_map/ppermute | solution.py:296
  17.0 2.1 %collective-permute-done.7 = bf16[1,64,512]{2,1,0:T(8,128)(2,1)S(1)} collective-permute-done((bf16[1,64,512]{2,1,0:T(8,128)(2,1)S(1)}, bf16[1,64,512]{2,1,0:T(8,128)(2,1)S(1)}, u32[]{:S(2)}, u32[]{:S(2)}) %collective-permute-start.7) | collective-permute-done | bytes 65568 | tf_op jit(solution)/shard_map/ppermute | solution.py:296
  19.0 1.6 %collective-permute-done.8 = bf16[1,64,512]{2,1,0:T(8,128)(2,1)S(1)} collective-permute-done((bf16[1,64,512]{2,1,0:T(8,128)(2,1)S(1)}, bf16[1,64,512]{2,1,0:T(8,128)(2,1)S(1)}, u32[]{:S(2)}, u32[]{:S(2)}) %collective-permute-start.8) | collective-permute-done | bytes 65568 | tf_op jit(solution)/shard_map/ppermute | solution.py:296
  20.6 0.0 collective-permute-done.9
  20.6 0.7 %fusion.1 = bf16[1,64,512]{2,1,0:T(8,128)(2,1)} fusion(bf16[1,64,512]{2,1,0:T(8,128)(2,1)S(1)} %collective-permute-done.9, bf16[1,64,512]{2,1,0:T(8,128)(2,1)S(1)} %collective-permute-done.8, f32[1,64,512]{2,1,0:T(8,128)S(1)} %get-tuple-element.37, bf16[1,64,512]{2,1,0:T(8,128)(2,1)S(1)} %collective-permute-done.7, f32[64,512]{1,0:T(8,128)S(1)} %get-tuple-element.26), kind=kLoop, calls=%fused_computation.2 | loop fusion | flops 294912 | bytes 524288 | tf_op jit(solution)/shard_map/broadcast_in_dim | solution.py:301
Async XLA Ops:
  1.0 7.6 %collective-permute-start.3 = (bf16[512,256]{1,0:T(8,128)(2,1)S(1)}, bf16[512,256]{1,0:T(8,128)(2,1)S(1)}, u32[]{:S(2)}, u32[]{:S(2)}) collective-permute-start(bf16[512,256]{1,0:T(8,128)(2,1)S(1)} %shard_map.64.refs_0_), channel_id=1, source_target_pairs={{0,9},{1,3},{2,11},{3,1},{4,13},{5,7},{6,15},{7,5},{8,17},{9,0},{1... | collective-permute-start | bytes 786440 | tf_op jit(solution)/shard_map/ppermute | solution.py:274
  3.5 7.5 %collective-permute-start.4 = (bf16[1,4,512,512]{3,2,1,0:T(8,128)(2,1)}, bf16[1,4,512,512]{3,2,1,0:T(8,128)(2,1)S(1)}, u32[]{:S(2)}, u32[]{:S(2)}) collective-permute-start(bf16[1,4,512,512]{3,2,1,0:T(8,128)(2,1)} %left_hbm), channel_id=1, source_target_pairs={{0,1},{1,0},{2,3},{3,2},{4,5},{5,4},{6,7},{7,6},{8,9},{9,8},{10,11... | collective-permute-start | bytes 6291464 | tf_op jit(solution)/shard_map/ppermute | solution.py:276
  3.5 7.5 %collective-permute-start.5 = (bf16[1,4,512,512]{3,2,1,0:T(8,128)(2,1)}, bf16[1,4,512,512]{3,2,1,0:T(8,128)(2,1)S(1)}, u32[]{:S(2)}, u32[]{:S(2)}) collective-permute-start(bf16[1,4,512,512]{3,2,1,0:T(8,128)(2,1)} %right_hbm), channel_id=1, source_target_pairs={{0,1},{1,0},{2,3},{3,2},{4,5},{5,4},{6,7},{7,6},{8,9},{9,8},{10,11... | collective-permute-start | bytes 6291464 | tf_op jit(solution)/shard_map/ppermute | solution.py:276
  5.0 5.9 %collective-permute-start = (bf16[512,256]{1,0:T(8,128)(2,1)S(1)}, bf16[512,256]{1,0:T(8,128)(2,1)S(1)}, u32[]{:S(2)}, u32[]{:S(2)}) collective-permute-start(bf16[512,256]{1,0:T(8,128)(2,1)S(1)} %shard_map.66.refs_0_), channel_id=1, source_target_pairs={{0,9},{1,3},{2,11},{3,1},{4,13},{5,7},{6,15},{7,5},{8,17},{9,0},{1... | collective-permute-start | bytes 786440 | tf_op jit(solution)/shard_map/ppermute | solution.py:274
  8.5 2.2 %collective-permute-start.1 = (s32[8,128]{1,0:T(8,128)S(1)}, s32[8,128]{1,0:T(8,128)S(1)}, u32[]{:S(2)}, u32[]{:S(2)}) collective-permute-start(s32[8,128]{1,0:T(8,128)S(1)} %get-tuple-element.31.refs_3_), channel_id=1, source_target_pairs={{0,1},{1,0},{2,3},{3,2},{4,5},{5,4},{6,7},{7,6},{8,9},{9,8},{10,11... | collective-permute-start | bytes 12296 | tf_op jit(solution)/shard_map/ppermute | solution.py:278
  8.6 2.5 %collective-permute-start.6 = (bf16[512,256]{1,0:T(8,128)(2,1)S(1)}, bf16[512,256]{1,0:T(8,128)(2,1)S(1)}, u32[]{:S(2)}, u32[]{:S(2)}) collective-permute-start(bf16[512,256]{1,0:T(8,128)(2,1)S(1)} %collective-permute-done.3.refs_1_), channel_id=1, source_target_pairs={{0,1},{1,0},{2,3},{3,2},{4,5},{5,4},{6,7},{7,6},{8,9},{9,8},{10,11... | collective-permute-start | bytes 786440 | tf_op jit(solution)/shard_map/ppermute | solution.py:281
  10.8 1.5 %collective-permute-start.2 = (bf16[512,256]{1,0:T(8,128)(2,1)S(1)}, bf16[512,256]{1,0:T(8,128)(2,1)S(1)}, u32[]{:S(2)}, u32[]{:S(2)}) collective-permute-start(bf16[512,256]{1,0:T(8,128)(2,1)S(1)} %collective-permute-done.refs_1_), channel_id=1, source_target_pairs={{0,1},{1,0},{2,3},{3,2},{4,5},{5,4},{6,7},{7,6},{8,9},{9,8},{10,11... | collective-permute-start | bytes 786440 | tf_op jit(solution)/shard_map/ppermute | solution.py:281
  13.7 5.3 %collective-permute-start.7 = (bf16[1,64,512]{2,1,0:T(8,128)(2,1)S(1)}, bf16[1,64,512]{2,1,0:T(8,128)(2,1)S(1)}, u32[]{:S(2)}, u32[]{:S(2)}) collective-permute-start(bf16[1,64,512]{2,1,0:T(8,128)(2,1)S(1)} %get-tuple-element.38), channel_id=1, source_target_pairs={{0,6},{1,7},{2,4},{3,5},{4,2},{5,3},{6,0},{7,1},{8,14},{9,15},{10,... | collective-permute-start | bytes 196616 | tf_op jit(solution)/shard_map/ppermute | solution.py:296
  16.5 4.2 %collective-permute-start.8 = (bf16[1,64,512]{2,1,0:T(8,128)(2,1)S(1)}, bf16[1,64,512]{2,1,0:T(8,128)(2,1)S(1)}, u32[]{:S(2)}, u32[]{:S(2)}) collective-permute-start(bf16[1,64,512]{2,1,0:T(8,128)(2,1)S(1)} %get-tuple-element.39), channel_id=1, source_target_pairs={{0,3},{1,2},{2,1},{3,0},{4,7},{5,6},{6,5},{7,4},{8,11},{9,10},{10,... | collective-permute-start | bytes 196616 | tf_op jit(solution)/shard_map/ppermute | solution.py:296
  16.7 4.0 %collective-permute-start.9 = (bf16[1,64,512]{2,1,0:T(8,128)(2,1)S(1)}, bf16[1,64,512]{2,1,0:T(8,128)(2,1)S(1)}, u32[]{:S(2)}, u32[]{:S(2)}) collective-permute-start(bf16[1,64,512]{2,1,0:T(8,128)(2,1)S(1)} %get-tuple-element.40), channel_id=1, source_target_pairs={{0,5},{1,4},{2,7},{3,6},{4,1},{5,0},{6,3},{7,2},{8,13},{9,12},{10,... | collective-permute-start | bytes 196616 | tf_op jit(solution)/shard_map/ppermute | solution.py:296

commit v6 on v5

--- a/solution.py
+++ b/solution.py
@@ -9,6 +9,7 @@
 
 AXES = ("sec", "mpo")
 CUTS = (256, 256)
+SHARES = ((3, 3), (4, 2), (2, 4))
 FLIPS = {4: (3, 1, 2), 2: (1,), 1: ()}
 VMEM = pl.BlockSpec(memory_space=pltpu.VMEM)
 HBM = pl.BlockSpec(memory_space=pltpu.HBM)
@@ -162,46 +163,76 @@
     return [pl.ds(pl.multiple_of(first, height), height) for first in firsts]
 
 
-def products(start, places, sources, groups, first_ref):
+def sources_first(code, terms):
+    active, picks = jnp.int32(0), [jnp.int32(0)] * terms
+    for wanted in (True, False):
+        for term in range(terms):
+            here = (((code >> (2 * term)) & 3) != 0) == wanted
+            picks = [jnp.where(here & (active == at), term, pick) for at, pick in enumerate(picks)]
+            active += jnp.where(here, 1, 0)
+        if wanted:
+            count = active
+    return count, picks
+
+
+def products(start, places, sources, groups, picked, first_ref):
     own, got, swapped = (ref[...] for ref in sources)
-    total = None
-    for code_ref, left_ref, right_ref, direct in groups:
+    width = own.shape[1]
+    rights, column = [], 0
+    for (code_ref, left_ref, right_ref, direct), picks in zip(groups, picked):
         code = code_ref[0, 0]
-        terms, order, _ = right_ref.shape
-        width = own.shape[1]
-        for term in range(terms):
+        for term in picks:
             choice = (code >> (2 * term)) & 3
             source = jnp.where(choice == direct, got, jnp.where(choice == 3 - direct, swapped, jnp.zeros_like(own)))
             source = jnp.where(choice == 3, own, source)
             left = left_ref[term] if places is None else jnp.concatenate([left_ref[term, at] for at in places], axis=0)
-            first_ref[:, term * width : (term + 1) * width] = dot(left, source).astype(jnp.bfloat16)
-        right = right_ref[:, start : start + width, :].reshape(terms * width, order)
-        total = dot(first_ref[...], right) if total is None else total + dot(first_ref[...], right)
-    return total
+            first_ref[:, column : column + width] = dot(left, source).astype(jnp.bfloat16)
+            column += width
+            rights.append(right_ref[term, start : start + width])
+    return dot(first_ref[:, :column], jnp.concatenate(rights, axis=0))
 
 
 def sums_kernel(start, group, height, flips, last, *refs):
     sources, (code, left, right, code_2, left_2, right_2), refs = refs[:3], refs[3:9], refs[9:]
-    order = left.shape[1]
+    terms, order, _ = left.shape
     groups = ((code, left, right, 2), (code_2, left_2.at[0], right_2.at[0], 1))
     places = row_blocks(group, height, flips)
     narrow = height % 16 == 0
     *before, first_ref, total_ref = refs[: -(2 + (1 + len(flips) if last else 1))] + refs[-2:]
     outs = refs[len(before) : -2]
-    total = products(start, places if narrow else None, sources, groups, first_ref)
-    for ref in before:
-        total += ref[...]
-    if not last:
-        outs[0][...] = total
-        return
-    if not narrow:
-        total_ref[...] = total
-    each = len(places) // len(outs)
-    for which, out_ref in enumerate(outs):
-        for at in range(each):
-            block = which * each + at
-            value = total[block * height : (block + 1) * height] if narrow else total_ref[places[block]]
-            out_ref[at] = value.astype(out_ref.dtype)
+
+    def run(picked):
+        total = products(start, places if narrow else None, sources, groups, picked, first_ref)
+        for ref in before:
+            total += ref[...]
+        if not last:
+            outs[0][...] = total
+            return
+        if not narrow:
+            total_ref[...] = total
+        each = len(places) // len(outs)
+        for which, out_ref in enumerate(outs):
+            for at in range(each):
+                block = which * each + at
+                value = total[block * height : (block + 1) * height] if narrow else total_ref[places[block]]
+                out_ref[at] = value.astype(out_ref.dtype)
+
+    (count, picks), (count_2, picks_2) = (sources_first(ref[0, 0], terms) for ref in (code, code_2))
+    taken = jnp.bool_(False)
+    for few in SHARES:
+        if terms != 4:
+            break
+        fits = (count <= few[0]) & (count_2 <= few[1])
+
+        @pl.when(fits & jnp.logical_not(taken))
+        def _():
+            run((picks[: few[0]], picks_2[: few[1]]))
+
+        taken = taken | fits
+
+    @pl.when(jnp.logical_not(taken))
+    def _():
+        run((range(terms), range(terms)))
 
 
 def sums(start, group, flips, last, sources, terms, before):
@@ -220,7 +251,7 @@
         out_specs=[VMEM] * len(outs),
         out_shape=outs,
         scratch_shapes=[
-            pltpu.VMEM((rows, count * sources[0].shape[1]), jnp.bfloat16),
+            pltpu.VMEM((rows, 2 * count * sources[0].shape[1]), jnp.bfloat16),
             pltpu.VMEM((order, order) if height % 16 else (8, 128), jnp.float32),
         ],
         compiler_params=PARAMS,

time: 21.6 us -> 21.6 us (level)
  Pallas kernels: 6.8 us -> 6.47 us
  waiting for transfers between devices: 5.64 us -> 5.97 us
    pallas_call x2, Pallas kernels: 2.64 us -> 2.32 us  [sums(): pl.pallas_call(functools.partial(sums_kernel, start, group, height, flips...]
  transfers between devices with their start and end apart: 10 -> 10, of which waited for: 5 -> 6; matrix products, arithmetic and copies ran while one was open for 0% -> 0% of each run, Pallas kernels for 21% -> 20%
where the time goes in v6:
time: 21.6 us; the launch traced here: 21.3 us
  starting transfers between devices  8.14 us (38%)
  Pallas kernels  6.47 us (30%)
  waiting for transfers between devices  5.97 us (28%)
  other arithmetic  0.68 us (3%)
    ppermute x3, waiting for transfers between devices, local(): lax.ppermute(sent, AXES, group_pairs(sectors, group, flip << 1 + bit | pa...  3.82 us
    ppermute x2, starting transfers between devices, local(): lax.ppermute(piece, AXES, halo_pairs(sectors, group))  3.78 us
    ppermute x3, starting transfers between devices, local(): lax.ppermute(sent, AXES, group_pairs(sectors, group, flip << 1 + bit | pa...  3.27 us
    pallas_call x2, Pallas kernels, sums(): pl.pallas_call(functools.partial(sums_kernel, start, group, height, flips...  2.32 us
    pallas_call x1, Pallas kernels, load(): pl.pallas_call(functools.partial(load_kernel, sectors), in_specs=[HBM] *...  2.24 us
    pallas_call x2, Pallas kernels, mask(): pl.pallas_call(functools.partial(mask_kernel, start), in_specs=[HBM, HBM]...  1.91 us
    ppermute x1, waiting for transfers between devices, local(): code_2 = lax.ppermute(code, AXES, to_core)  1.61 us
    broadcast_in_dim x1, other arithmetic, local(): return value.astype(jnp.bfloat16)[None]  0.68 us
  transfers between devices with their start and end apart: 10, of which 6 were waited for; matrix products, arithmetic and copies ran while one was open for 0% of the time, Pallas kernels for 20%

profile of v6, /device:TPU:0, one launch (start us, length us, event | category | flops | bytes accessed | tf_op | source)
XLA Modules:
  0.0 21.3 jit_solution(17270536604431587868)
XLA Ops:
  0.0 1.0 %shard_map.64.refs_0_ = bf16[512,256]{1,0:T(8,128)(2,1)S(1)} custom-call(s32[1,2]{1,0:T(1,128)} %dims_hbm.5, bf16[1,512,512]{2,1,0:T(8,128)(2,1)} %psi_hbm.2), custom_call_target="tpu_custom_call" | custom-call | tf_op jit(solution)/shard_map/pallas_call | solution.py:84
  1.0 2.5 %collective-permute-start.3 = (bf16[512,256]{1,0:T(8,128)(2,1)S(1)}, bf16[512,256]{1,0:T(8,128)(2,1)S(1)}, u32[]{:S(2)}, u32[]{:S(2)}) collective-permute-start(bf16[512,256]{1,0:T(8,128)(2,1)S(1)} %shard_map.64.refs_0_), channel_id=1, source_target_pairs={{0,9},{1,3},{2,11},{3,1},{4,13},{5,7},{6,15},{7,5},{8,17},{9,0},{1... | collective-permute-start | bytes 786440 | tf_op jit(solution)/shard_map/ppermute | solution.py:305
  3.5 0.0 collective-permute-start.4
  3.5 0.5 %collective-permute-start.5 = (bf16[1,4,512,512]{3,2,1,0:T(8,128)(2,1)}, bf16[1,4,512,512]{3,2,1,0:T(8,128)(2,1)S(1)}, u32[]{:S(2)}, u32[]{:S(2)}) collective-permute-start(bf16[1,4,512,512]{3,2,1,0:T(8,128)(2,1)} %right_hbm), channel_id=1, source_target_pairs={{0,1},{1,0},{2,3},{3,2},{4,5},{5,4},{6,7},{7,6},{8,9},{9,8},{10,11... | collective-permute-start | bytes 6291464 | tf_op jit(solution)/shard_map/ppermute | solution.py:307
  4.0 1.0 %shard_map.66.refs_0_ = bf16[512,256]{1,0:T(8,128)(2,1)S(1)} custom-call(s32[1,2]{1,0:T(1,128)} %dims_hbm.5, bf16[1,512,512]{2,1,0:T(8,128)(2,1)} %psi_hbm.2), custom_call_target="tpu_custom_call" | custom-call | flops 49999998976 | tf_op jit(solution)/shard_map/pallas_call | solution.py:84
  5.0 1.2 %collective-permute-start = (bf16[512,256]{1,0:T(8,128)(2,1)S(1)}, bf16[512,256]{1,0:T(8,128)(2,1)S(1)}, u32[]{:S(2)}, u32[]{:S(2)}) collective-permute-start(bf16[512,256]{1,0:T(8,128)(2,1)S(1)} %shard_map.66.refs_0_), channel_id=1, source_target_pairs={{0,9},{1,3},{2,11},{3,1},{4,13},{5,7},{6,15},{7,5},{8,17},{9,0},{1... | collective-permute-start | bytes 786440 | tf_op jit(solution)/shard_map/ppermute | solution.py:305
  6.2 2.2 %shard_map.65 = (bf16[4,512,512]{2,1,0:T(8,128)(2,1)S(1)}, bf16[4,512,512]{2,1,0:T(8,128)(2,1)S(1)}, s32[8,128]{1,0:T(8,128)S(1)}, f32[64,512]{1,0:T(8,128)S(1)}) custom-call(s32[1,2]{1,0:T(1,128)} %dims_hbm.5, s32[4]{0:T(128)} %shift_hbm.1, s32[1,4]{1,0:T(1,128)} %connect_hbm.1, bf16[1,4,512,512]{3,2,1,0:T(8,128)(2,1)} %left_hbm, ...), custom_call_target="tpu_custom_call" | custom-call | flops 2147483648 | bytes 4194304 | tf_op jit(solution)/shard_map/pallas_call | solution.py:133
  8.5 0.1 collective-permute-start.1
  8.6 0.0 collective-permute-done.3.refs_1_
  8.6 0.5 %collective-permute-start.6 = (bf16[512,256]{1,0:T(8,128)(2,1)S(1)}, bf16[512,256]{1,0:T(8,128)(2,1)S(1)}, u32[]{:S(2)}, u32[]{:S(2)}) collective-permute-start(bf16[512,256]{1,0:T(8,128)(2,1)S(1)} %collective-permute-done.3.refs_1_), channel_id=1, source_target_pairs={{0,1},{1,0},{2,3},{3,2},{4,5},{5,4},{6,7},{7,6},{8,9},{9,8},{10,11... | collective-permute-start | bytes 786440 | tf_op jit(solution)/shard_map/ppermute | solution.py:312
  9.0 1.6 %collective-permute-done.1.refs_6_ = s32[8,128]{1,0:T(8,128)S(1)} collective-permute-done((s32[8,128]{1,0:T(8,128)S(1)}, s32[8,128]{1,0:T(8,128)S(1)}, u32[]{:S(2)}, u32[]{:S(2)}) %collective-permute-start.1) | collective-permute-done | bytes 4128 | tf_op jit(solution)/shard_map/ppermute | solution.py:309
  10.7 0.2 collective-permute-done.refs_1_
  10.8 0.0 collective-permute-start.2
  10.8 0.2 collective-permute-done.6.refs_2_
  11.0 0.0 collective-permute-done.4.refs_7_
  11.0 0.0 collective-permute-done.5.refs_8_
  11.0 1.2 %shard_map.67.refs_9_ = f32[256,512]{1,0:T(8,128)S(1)} custom-call(bf16[512,256]{1,0:T(8,128)(2,1)S(1)} %shard_map.64.refs_0_, bf16[512,256]{1,0:T(8,128)(2,1)S(1)} %collective-permute-done.3.refs_1_, bf16[512,256]{1,0:T(8,128)(2,1)S(1)} %collective-permute-done.6.refs_2_, s32[8,128]{1,0:T(8,128)S(1)} %get-tuple-element.31.refs_3_, ...), custom_call_target="tpu_custom_call" | custom-call | tf_op jit(solution)/shard_map/pallas_call | solution.py:248
  12.2 0.2 collective-permute-done.2.refs_2_
  12.4 1.2 %shard_map.68 = (f32[1,64,512]{2,1,0:T(8,128)S(1)}, bf16[1,64,512]{2,1,0:T(8,128)(2,1)S(1)}, bf16[1,64,512]{2,1,0:T(8,128)(2,1)S(1)}, bf16[1,64,512]{2,1,0:T(8,128)(2,1)S(1)}) custom-call(bf16[512,256]{1,0:T(8,128)(2,1)S(1)} %shard_map.66.refs_0_, bf16[512,256]{1,0:T(8,128)(2,1)S(1)} %collective-permute-done.refs_1_, ...), custom_call_target="tpu_custom_call" | custom-call | tf_op jit(solution)/shard_map/pallas_call | solution.py:248
  13.5 2.8 %collective-permute-start.7 = (bf16[1,64,512]{2,1,0:T(8,128)(2,1)S(1)}, bf16[1,64,512]{2,1,0:T(8,128)(2,1)S(1)}, u32[]{:S(2)}, u32[]{:S(2)}) collective-permute-start(bf16[1,64,512]{2,1,0:T(8,128)(2,1)S(1)} %get-tuple-element.38), channel_id=1, source_target_pairs={{0,6},{1,7},{2,4},{3,5},{4,2},{5,3},{6,0},{7,1},{8,14},{9,15},{10,... | collective-permute-start | bytes 196616 | tf_op jit(solution)/shard_map/ppermute | solution.py:327
  16.3 0.0 collective-permute-start.8
  16.3 0.5 %collective-permute-start.9 = (bf16[1,64,512]{2,1,0:T(8,128)(2,1)S(1)}, bf16[1,64,512]{2,1,0:T(8,128)(2,1)S(1)}, u32[]{:S(2)}, u32[]{:S(2)}) collective-permute-start(bf16[1,64,512]{2,1,0:T(8,128)(2,1)S(1)} %get-tuple-element.40), channel_id=1, source_target_pairs={{0,5},{1,4},{2,7},{3,6},{4,1},{5,0},{6,3},{7,2},{8,13},{9,12},{10,... | collective-permute-start | bytes 196616 | tf_op jit(solution)/shard_map/ppermute | solution.py:327
  16.8 2.0 %collective-permute-done.7 = bf16[1,64,512]{2,1,0:T(8,128)(2,1)S(1)} collective-permute-done((bf16[1,64,512]{2,1,0:T(8,128)(2,1)S(1)}, bf16[1,64,512]{2,1,0:T(8,128)(2,1)S(1)}, u32[]{:S(2)}, u32[]{:S(2)}) %collective-permute-start.7) | collective-permute-done | bytes 65568 | tf_op jit(solution)/shard_map/ppermute | solution.py:327
  18.8 1.9 %collective-permute-done.8 = bf16[1,64,512]{2,1,0:T(8,128)(2,1)S(1)} collective-permute-done((bf16[1,64,512]{2,1,0:T(8,128)(2,1)S(1)}, bf16[1,64,512]{2,1,0:T(8,128)(2,1)S(1)}, u32[]{:S(2)}, u32[]{:S(2)}) %collective-permute-start.8) | collective-permute-done | bytes 65568 | tf_op jit(solution)/shard_map/ppermute | solution.py:327
  20.6 0.0 collective-permute-done.9
  20.6 0.7 %fusion.1 = bf16[1,64,512]{2,1,0:T(8,128)(2,1)} fusion(bf16[1,64,512]{2,1,0:T(8,128)(2,1)S(1)} %collective-permute-done.9, bf16[1,64,512]{2,1,0:T(8,128)(2,1)S(1)} %collective-permute-done.8, f32[1,64,512]{2,1,0:T(8,128)S(1)} %get-tuple-element.37, bf16[1,64,512]{2,1,0:T(8,128)(2,1)S(1)} %collective-permute-done.7, f32[64,512]{1,0:T(8,128)S(1)} %get-tuple-element.26), kind=kLoop, calls=%fused_computation.2 | loop fusion | flops 294912 | bytes 524288 | tf_op jit(solution)/shard_map/broadcast_in_dim | solution.py:332
Async XLA Ops:
  1.0 7.6 %collective-permute-start.3 = (bf16[512,256]{1,0:T(8,128)(2,1)S(1)}, bf16[512,256]{1,0:T(8,128)(2,1)S(1)}, u32[]{:S(2)}, u32[]{:S(2)}) collective-permute-start(bf16[512,256]{1,0:T(8,128)(2,1)S(1)} %shard_map.64.refs_0_), channel_id=1, source_target_pairs={{0,9},{1,3},{2,11},{3,1},{4,13},{5,7},{6,15},{7,5},{8,17},{9,0},{1... | collective-permute-start | bytes 786440 | tf_op jit(solution)/shard_map/ppermute | solution.py:305
  3.5 7.5 %collective-permute-start.4 = (bf16[1,4,512,512]{3,2,1,0:T(8,128)(2,1)}, bf16[1,4,512,512]{3,2,1,0:T(8,128)(2,1)S(1)}, u32[]{:S(2)}, u32[]{:S(2)}) collective-permute-start(bf16[1,4,512,512]{3,2,1,0:T(8,128)(2,1)} %left_hbm), channel_id=1, source_target_pairs={{0,1},{1,0},{2,3},{3,2},{4,5},{5,4},{6,7},{7,6},{8,9},{9,8},{10,11... | collective-permute-start | bytes 6291464 | tf_op jit(solution)/shard_map/ppermute | solution.py:307
  3.5 7.5 %collective-permute-start.5 = (bf16[1,4,512,512]{3,2,1,0:T(8,128)(2,1)}, bf16[1,4,512,512]{3,2,1,0:T(8,128)(2,1)S(1)}, u32[]{:S(2)}, u32[]{:S(2)}) collective-permute-start(bf16[1,4,512,512]{3,2,1,0:T(8,128)(2,1)} %right_hbm), channel_id=1, source_target_pairs={{0,1},{1,0},{2,3},{3,2},{4,5},{5,4},{6,7},{7,6},{8,9},{9,8},{10,11... | collective-permute-start | bytes 6291464 | tf_op jit(solution)/shard_map/ppermute | solution.py:307
  5.0 5.9 %collective-permute-start = (bf16[512,256]{1,0:T(8,128)(2,1)S(1)}, bf16[512,256]{1,0:T(8,128)(2,1)S(1)}, u32[]{:S(2)}, u32[]{:S(2)}) collective-permute-start(bf16[512,256]{1,0:T(8,128)(2,1)S(1)} %shard_map.66.refs_0_), channel_id=1, source_target_pairs={{0,9},{1,3},{2,11},{3,1},{4,13},{5,7},{6,15},{7,5},{8,17},{9,0},{1... | collective-permute-start | bytes 786440 | tf_op jit(solution)/shard_map/ppermute | solution.py:305
  8.5 2.2 %collective-permute-start.1 = (s32[8,128]{1,0:T(8,128)S(1)}, s32[8,128]{1,0:T(8,128)S(1)}, u32[]{:S(2)}, u32[]{:S(2)}) collective-permute-start(s32[8,128]{1,0:T(8,128)S(1)} %get-tuple-element.31.refs_3_), channel_id=1, source_target_pairs={{0,1},{1,0},{2,3},{3,2},{4,5},{5,4},{6,7},{7,6},{8,9},{9,8},{10,11... | collective-permute-start | bytes 12296 | tf_op jit(solution)/shard_map/ppermute | solution.py:309
  8.6 2.5 %collective-permute-start.6 = (bf16[512,256]{1,0:T(8,128)(2,1)S(1)}, bf16[512,256]{1,0:T(8,128)(2,1)S(1)}, u32[]{:S(2)}, u32[]{:S(2)}) collective-permute-start(bf16[512,256]{1,0:T(8,128)(2,1)S(1)} %collective-permute-done.3.refs_1_), channel_id=1, source_target_pairs={{0,1},{1,0},{2,3},{3,2},{4,5},{5,4},{6,7},{7,6},{8,9},{9,8},{10,11... | collective-permute-start | bytes 786440 | tf_op jit(solution)/shard_map/ppermute | solution.py:312
  10.8 1.5 %collective-permute-start.2 = (bf16[512,256]{1,0:T(8,128)(2,1)S(1)}, bf16[512,256]{1,0:T(8,128)(2,1)S(1)}, u32[]{:S(2)}, u32[]{:S(2)}) collective-permute-start(bf16[512,256]{1,0:T(8,128)(2,1)S(1)} %collective-permute-done.refs_1_), channel_id=1, source_target_pairs={{0,1},{1,0},{2,3},{3,2},{4,5},{5,4},{6,7},{7,6},{8,9},{9,8},{10,11... | collective-permute-start | bytes 786440 | tf_op jit(solution)/shard_map/ppermute | solution.py:312
  13.5 5.2 %collective-permute-start.7 = (bf16[1,64,512]{2,1,0:T(8,128)(2,1)S(1)}, bf16[1,64,512]{2,1,0:T(8,128)(2,1)S(1)}, u32[]{:S(2)}, u32[]{:S(2)}) collective-permute-start(bf16[1,64,512]{2,1,0:T(8,128)(2,1)S(1)} %get-tuple-element.38), channel_id=1, source_target_pairs={{0,6},{1,7},{2,4},{3,5},{4,2},{5,3},{6,0},{7,1},{8,14},{9,15},{10,... | collective-permute-start | bytes 196616 | tf_op jit(solution)/shard_map/ppermute | solution.py:327
  16.3 4.3 %collective-permute-start.8 = (bf16[1,64,512]{2,1,0:T(8,128)(2,1)S(1)}, bf16[1,64,512]{2,1,0:T(8,128)(2,1)S(1)}, u32[]{:S(2)}, u32[]{:S(2)}) collective-permute-start(bf16[1,64,512]{2,1,0:T(8,128)(2,1)S(1)} %get-tuple-element.39), channel_id=1, source_target_pairs={{0,3},{1,2},{2,1},{3,0},{4,7},{5,6},{6,5},{7,4},{8,11},{9,10},{10,... | collective-permute-start | bytes 196616 | tf_op jit(solution)/shard_map/ppermute | solution.py:327
  16.3 4.3 %collective-permute-start.9 = (bf16[1,64,512]{2,1,0:T(8,128)(2,1)S(1)}, bf16[1,64,512]{2,1,0:T(8,128)(2,1)S(1)}, u32[]{:S(2)}, u32[]{:S(2)}) collective-permute-start(bf16[1,64,512]{2,1,0:T(8,128)(2,1)S(1)} %get-tuple-element.40), channel_id=1, source_target_pairs={{0,5},{1,4},{2,7},{3,6},{4,1},{5,0},{6,3},{7,2},{8,13},{9,12},{10,... | collective-permute-start | bytes 196616 | tf_op jit(solution)/shard_map/ppermute | solution.py:327

commit v7 on v6

--- a/solution.py
+++ b/solution.py
@@ -9,7 +9,7 @@
 
 AXES = ("sec", "mpo")
 CUTS = (256, 256)
-SHARES = ((3, 3), (4, 2), (2, 4))
+SHARES = {False: (), True: ((2, 4), (3, 3))}
 FLIPS = {4: (3, 1, 2), 2: (1,), 1: ()}
 VMEM = pl.BlockSpec(memory_space=pltpu.VMEM)
 HBM = pl.BlockSpec(memory_space=pltpu.HBM)
@@ -179,8 +179,7 @@
     own, got, swapped = (ref[...] for ref in sources)
     width = own.shape[1]
     rights, column = [], 0
-    for (code_ref, left_ref, right_ref, direct), picks in zip(groups, picked):
-        code = code_ref[0, 0]
+    for (code, left_ref, right_ref, direct), picks in zip(groups, picked):
         for term in picks:
             choice = (code >> (2 * term)) & 3
             source = jnp.where(choice == direct, got, jnp.where(choice == 3 - direct, swapped, jnp.zeros_like(own)))
@@ -190,6 +189,33 @@
             column += width
             rights.append(right_ref[term, start : start + width])
     return dot(first_ref[:, :column], jnp.concatenate(rights, axis=0))
+
+
+def own_kernel(start, group, height, flips, own_ref, code_ref, left_ref, right_ref, total_ref, first_ref):
+    places = row_blocks(group, height, flips)
+    own, code = own_ref[...], code_ref[0, 0]
+    terms, order, _ = left_ref.shape
+    width = own.shape[1]
+    for term in range(terms):
+        source = jnp.where((code >> (2 * term)) & 3 == 3, own, jnp.zeros_like(own))
+        left = left_ref[term] if height % 16 else jnp.concatenate([left_ref[term, at] for at in places], axis=0)
+        first_ref[:, term * width : (term + 1) * width] = dot(left, source).astype(jnp.bfloat16)
+    right = right_ref[:, start : start + width, :].reshape(terms * width, order)
+    total_ref[...] = dot(first_ref[...], right)
+
+
+def own_sums(start, group, flips, own, code, left, right):
+    terms, order, _ = left.shape
+    height = order // group
+    rows = order // 2 if height % 16 == 0 else order
+    return pl.pallas_call(
+        functools.partial(own_kernel, start, group, height, flips),
+        in_specs=[VMEM] * 4,
+        out_specs=VMEM,
+        out_shape=pltpu.VMEM((rows, order), jnp.float32),
+        scratch_shapes=[pltpu.VMEM((rows, terms * own.shape[1]), jnp.bfloat16)],
+        compiler_params=PARAMS,
+    )(own, code, left, right)
 
 
 def sums_kernel(start, group, height, flips, last, *refs):
@@ -217,9 +243,15 @@
                 value = total[block * height : (block + 1) * height] if narrow else total_ref[places[block]]
                 out_ref[at] = value.astype(out_ref.dtype)
 
-    (count, picks), (count_2, picks_2) = (sources_first(ref[0, 0], terms) for ref in (code, code_2))
+    numbers = [code[0, 0], code_2[0, 0]]
+    if last:
+        for term in range(terms):
+            here = 3 << (2 * term)
+            numbers[0] = jnp.where(numbers[0] & here == here, numbers[0] & ~here, numbers[0])
+    groups = tuple((number, *rest) for number, (_, *rest) in zip(numbers, groups))
+    (count, picks), (count_2, picks_2) = (sources_first(number, terms) for number in numbers)
     taken = jnp.bool_(False)
-    for few in SHARES:
+    for few in SHARES[last]:
         if terms != 4:
             break
         fits = (count <= few[0]) & (count_2 <= few[1])
@@ -307,13 +339,15 @@
     left_2, right_2 = (lax.ppermute(env, AXES, to_core) for env in (left_env, right_env))
     left, right, code, keep = load(sectors, group, dims, term_shift, connect, left_env, right_env)
     code_2 = lax.ppermute(code, AXES, to_core)
-    got[0], code = lax.optimization_barrier((got[0], code))
+    flips = FLIPS[stages_of(group)[0][1]]
+    early = own_sums(sum(CUTS[:-1]), group, flips, pieces[-1], code, left, right)
+    got[0], code, early = lax.optimization_barrier((got[0], code, early))
     got[-1], code_2 = lax.optimization_barrier((got[-1], code_2))
     swapped = [lax.ppermute(piece, AXES, to_core) for piece in got]
 
     terms = (code, left, right, code_2, left_2, right_2)
     stages = stages_of(group)
-    start, addends = 0, []
+    start, addends = 0, [early]
     for at, cut in enumerate(CUTS):
         last = at == len(CUTS) - 1
         addends = sums(start, group, FLIPS[stages[0][1]], last, (pieces[at], got[at], swapped[at]), terms, addends)

time: 21.6 us -> 21.4 us (level)
  waiting for transfers between devices: 5.97 us -> 4.76 us
  Pallas kernels: 6.47 us -> 7.4 us
    ppermute x1, waiting for transfers between devices: 1.61 us -> 0.79 us  [local(): code_2 = lax.ppermute(code, AXES, to_core)]
    pallas_call x0 -> x1, Pallas kernels: none -> 0.74 us  [own_sums(): pl.pallas_call(functools.partial(own_kernel, start, group, height, flips)...]
    ppermute x3, waiting for transfers between devices: 3.82 us -> 3.59 us  [local(): lax.ppermute(sent, AXES, group_pairs(sectors, group, flip << 1 + bit | pa...]
  transfers between devices with their start and end apart: 10 -> 10, of which waited for: 6 -> 5; matrix products, arithmetic and copies ran while one was open for 0% -> 0% of each run, Pallas kernels for 20% -> 25%
where the time goes in v7:
time: 21.4 us; the launch traced here: 21.1 us
  starting transfers between devices  8.22 us (38%)
  Pallas kernels  7.4 us (35%)
  waiting for transfers between devices  4.76 us (22%)
  other arithmetic  0.68 us (3%)
    ppermute x2, starting transfers between devices, local(): lax.ppermute(piece, AXES, halo_pairs(sectors, group))  3.78 us
    ppermute x3, waiting for transfers between devices, local(): lax.ppermute(sent, AXES, group_pairs(sectors, group, flip << 1 + bit | pa...  3.59 us
    ppermute x3, starting transfers between devices, local(): lax.ppermute(sent, AXES, group_pairs(sectors, group, flip << 1 + bit | pa...  3.29 us
    pallas_call x2, Pallas kernels, sums(): pl.pallas_call(functools.partial(sums_kernel, start, group, height, flips...  2.51 us
    pallas_call x1, Pallas kernels, load(): pl.pallas_call(functools.partial(load_kernel, sectors), in_specs=[HBM] *...  2.24 us
    pallas_call x2, Pallas kernels, mask(): pl.pallas_call(functools.partial(mask_kernel, start), in_specs=[HBM, HBM]...  1.91 us
    ppermute x1, waiting for transfers between devices, local(): code_2 = lax.ppermute(code, AXES, to_core)  0.79 us
    pallas_call x1, Pallas kernels, own_sums(): pl.pallas_call(functools.partial(own_kernel, start, group, height, flips)...  0.74 us
  transfers between devices with their start and end apart: 10, of which 5 were waited for; matrix products, arithmetic and copies ran while one was open for 0% of the time, Pallas kernels for 25%

profile of v7, /device:TPU:0, one launch (start us, length us, event | category | flops | bytes accessed | tf_op | source)
XLA Modules:
  0.0 21.1 jit_solution(1851687530759951593)
XLA Ops:
  0.0 1.0 %shard_map.64.refs_0_ = bf16[512,256]{1,0:T(8,128)(2,1)S(1)} custom-call(s32[1,2]{1,0:T(1,128)} %dims_hbm.5, bf16[1,512,512]{2,1,0:T(8,128)(2,1)} %psi_hbm.2), custom_call_target="tpu_custom_call" | custom-call | tf_op jit(solution)/shard_map/pallas_call | solution.py:84
  1.0 2.5 %collective-permute-start.3 = (bf16[512,256]{1,0:T(8,128)(2,1)S(1)}, bf16[512,256]{1,0:T(8,128)(2,1)S(1)}, u32[]{:S(2)}, u32[]{:S(2)}) collective-permute-start(bf16[512,256]{1,0:T(8,128)(2,1)S(1)} %shard_map.64.refs_0_), channel_id=1, source_target_pairs={{0,9},{1,3},{2,11},{3,1},{4,13},{5,7},{6,15},{7,5},{8,17},{9,0},{1... | collective-permute-start | bytes 786440 | tf_op jit(solution)/shard_map/ppermute | solution.py:337
  3.5 0.0 collective-permute-start.4
  3.5 0.5 %collective-permute-start.5 = (bf16[1,4,512,512]{3,2,1,0:T(8,128)(2,1)}, bf16[1,4,512,512]{3,2,1,0:T(8,128)(2,1)S(1)}, u32[]{:S(2)}, u32[]{:S(2)}) collective-permute-start(bf16[1,4,512,512]{3,2,1,0:T(8,128)(2,1)} %right_hbm), channel_id=1, source_target_pairs={{0,1},{1,0},{2,3},{3,2},{4,5},{5,4},{6,7},{7,6},{8,9},{9,8},{10,11... | collective-permute-start | bytes 6291464 | tf_op jit(solution)/shard_map/ppermute | solution.py:339
  4.0 1.0 %shard_map.66.own_ref.refs_0_ = bf16[512,256]{1,0:T(8,128)(2,1)S(1)} custom-call(s32[1,2]{1,0:T(1,128)} %dims_hbm.5, bf16[1,512,512]{2,1,0:T(8,128)(2,1)} %psi_hbm.2), custom_call_target="tpu_custom_call" | custom-call | flops 49999998976 | tf_op jit(solution)/shard_map/pallas_call | solution.py:84
  5.0 1.2 %collective-permute-start = (bf16[512,256]{1,0:T(8,128)(2,1)S(1)}, bf16[512,256]{1,0:T(8,128)(2,1)S(1)}, u32[]{:S(2)}, u32[]{:S(2)}) collective-permute-start(bf16[512,256]{1,0:T(8,128)(2,1)S(1)} %shard_map.66.own_ref.refs_0_), channel_id=1, source_target_pairs={{0,9},{1,3},{2,11},{3,1},{4,13},{5,7},{6,15},{7,5},{8,17},{9,0},{1... | collective-permute-start | bytes 786440 | tf_op jit(solution)/shard_map/ppermute | solution.py:337
  6.2 2.2 %shard_map.65 = (bf16[4,512,512]{2,1,0:T(8,128)(2,1)S(1)}, bf16[4,512,512]{2,1,0:T(8,128)(2,1)S(1)}, s32[8,128]{1,0:T(8,128)S(1)}, f32[64,512]{1,0:T(8,128)S(1)}) custom-call(s32[1,2]{1,0:T(1,128)} %dims_hbm.5, s32[4]{0:T(128)} %shift_hbm.1, s32[1,4]{1,0:T(1,128)} %connect_hbm.1, bf16[1,4,512,512]{3,2,1,0:T(8,128)(2,1)} %left_hbm, ...), custom_call_target="tpu_custom_call" | custom-call | flops 2147483648 | bytes 4194304 | tf_op jit(solution)/shard_map/pallas_call | solution.py:133
  8.5 0.1 collective-permute-start.1
  8.6 0.7 %shard_map.67.refs_9_ = f32[256,512]{1,0:T(8,128)S(1)} custom-call(bf16[512,256]{1,0:T(8,128)(2,1)S(1)} %shard_map.66.own_ref.refs_0_, s32[8,128]{1,0:T(8,128)S(1)} %get-tuple-element.34.code_ref.refs_3_, bf16[4,512,512]{2,1,0:T(8,128)(2,1)S(1)} %get-tuple-element.32.left_ref.refs_4_, bf16[4,512,512]{2,1,0:T(8,128)(2,1)S(1)} %get-tuple-element.33.right_ref.refs_5_), custom_call_target="tpu_custom_call" | custom-call | tf_op jit(solution)/shard_map/pallas_call | solution.py:211
  9.3 0.0 collective-permute-done.3.refs_1_
  9.3 0.5 %collective-permute-start.6 = (bf16[512,256]{1,0:T(8,128)(2,1)S(1)}, bf16[512,256]{1,0:T(8,128)(2,1)S(1)}, u32[]{:S(2)}, u32[]{:S(2)}) collective-permute-start(bf16[512,256]{1,0:T(8,128)(2,1)S(1)} %collective-permute-done.3.refs_1_), channel_id=1, source_target_pairs={{0,1},{1,0},{2,3},{3,2},{4,5},{5,4},{6,7},{7,6},{8,9},{9,8},{10,11... | collective-permute-start | bytes 786440 | tf_op jit(solution)/shard_map/ppermute | solution.py:346
  9.9 0.8 %collective-permute-done.1.refs_6_ = s32[8,128]{1,0:T(8,128)S(1)} collective-permute-done((s32[8,128]{1,0:T(8,128)S(1)}, s32[8,128]{1,0:T(8,128)S(1)}, u32[]{:S(2)}, u32[]{:S(2)}) %collective-permute-start.1) | collective-permute-done | bytes 4128 | tf_op jit(solution)/shard_map/ppermute | solution.py:341
  10.7 0.2 collective-permute-done.refs_1_
  10.8 0.0 collective-permute-start.2
  10.8 0.2 collective-permute-done.6.refs_2_
  11.0 0.0 collective-permute-done.4.refs_7_
  11.0 0.0 collective-permute-done.5.refs_8_
  11.0 1.3 %shard_map.68.refs_9_ = f32[256,512]{1,0:T(8,128)S(1)} custom-call(bf16[512,256]{1,0:T(8,128)(2,1)S(1)} %shard_map.64.refs_0_, bf16[512,256]{1,0:T(8,128)(2,1)S(1)} %collective-permute-done.3.refs_1_, bf16[512,256]{1,0:T(8,128)(2,1)S(1)} %collective-permute-done.6.refs_2_, s32[8,128]{1,0:T(8,128)S(1)} %get-tuple-element.34.code_ref.refs_3_, ...), custom_call_target="tpu_custom_call" | custom-call | tf_op jit(solution)/shard_map/pallas_call | solution.py:280
  12.4 0.0 collective-permute-done.2.refs_2_
  12.4 1.2 %shard_map.69 = (f32[1,64,512]{2,1,0:T(8,128)S(1)}, bf16[1,64,512]{2,1,0:T(8,128)(2,1)S(1)}, bf16[1,64,512]{2,1,0:T(8,128)(2,1)S(1)}, bf16[1,64,512]{2,1,0:T(8,128)(2,1)S(1)}) custom-call(bf16[512,256]{1,0:T(8,128)(2,1)S(1)} %shard_map.66.own_ref.refs_0_, bf16[512,256]{1,0:T(8,128)(2,1)S(1)} %collective-permute-done.refs_1_, ...), custom_call_target="tpu_custom_call" | custom-call | tf_op jit(solution)/shard_map/pallas_call | solution.py:280
  13.6 2.7 %collective-permute-start.7 = (bf16[1,64,512]{2,1,0:T(8,128)(2,1)S(1)}, bf16[1,64,512]{2,1,0:T(8,128)(2,1)S(1)}, u32[]{:S(2)}, u32[]{:S(2)}) collective-permute-start(bf16[1,64,512]{2,1,0:T(8,128)(2,1)S(1)} %get-tuple-element.40), channel_id=1, source_target_pairs={{0,6},{1,7},{2,4},{3,5},{4,2},{5,3},{6,0},{7,1},{8,14},{9,15},{10,... | collective-permute-start | bytes 196616 | tf_op jit(solution)/shard_map/ppermute | solution.py:361
  16.3 0.2 collective-permute-start.8
  16.5 0.3 %collective-permute-start.9 = (bf16[1,64,512]{2,1,0:T(8,128)(2,1)S(1)}, bf16[1,64,512]{2,1,0:T(8,128)(2,1)S(1)}, u32[]{:S(2)}, u32[]{:S(2)}) collective-permute-start(bf16[1,64,512]{2,1,0:T(8,128)(2,1)S(1)} %get-tuple-element.42), channel_id=1, source_target_pairs={{0,5},{1,4},{2,7},{3,6},{4,1},{5,0},{6,3},{7,2},{8,13},{9,12},{10,... | collective-permute-start | bytes 196616 | tf_op jit(solution)/shard_map/ppermute | solution.py:361
  16.9 2.0 %collective-permute-done.7 = bf16[1,64,512]{2,1,0:T(8,128)(2,1)S(1)} collective-permute-done((bf16[1,64,512]{2,1,0:T(8,128)(2,1)S(1)}, bf16[1,64,512]{2,1,0:T(8,128)(2,1)S(1)}, u32[]{:S(2)}, u32[]{:S(2)}) %collective-permute-start.7) | collective-permute-done | bytes 65568 | tf_op jit(solution)/shard_map/ppermute | solution.py:361
  18.9 1.5 %collective-permute-done.8 = bf16[1,64,512]{2,1,0:T(8,128)(2,1)S(1)} collective-permute-done((bf16[1,64,512]{2,1,0:T(8,128)(2,1)S(1)}, bf16[1,64,512]{2,1,0:T(8,128)(2,1)S(1)}, u32[]{:S(2)}, u32[]{:S(2)}) %collective-permute-start.8) | collective-permute-done | bytes 65568 | tf_op jit(solution)/shard_map/ppermute | solution.py:361
  20.5 0.0 collective-permute-done.9
  20.5 0.7 %fusion.1 = bf16[1,64,512]{2,1,0:T(8,128)(2,1)} fusion(bf16[1,64,512]{2,1,0:T(8,128)(2,1)S(1)} %collective-permute-done.9, bf16[1,64,512]{2,1,0:T(8,128)(2,1)S(1)} %collective-permute-done.8, f32[1,64,512]{2,1,0:T(8,128)S(1)} %get-tuple-element.39, bf16[1,64,512]{2,1,0:T(8,128)(2,1)S(1)} %collective-permute-done.7, f32[64,512]{1,0:T(8,128)S(1)} %get-tuple-element.27), kind=kLoop, calls=%fused_computation.2 | loop fusion | flops 294912 | bytes 524288 | tf_op jit(solution)/shard_map/broadcast_in_dim | solution.py:366
Async XLA Ops:
  1.0 8.4 %collective-permute-start.3 = (bf16[512,256]{1,0:T(8,128)(2,1)S(1)}, bf16[512,256]{1,0:T(8,128)(2,1)S(1)}, u32[]{:S(2)}, u32[]{:S(2)}) collective-permute-start(bf16[512,256]{1,0:T(8,128)(2,1)S(1)} %shard_map.64.refs_0_), channel_id=1, source_target_pairs={{0,9},{1,3},{2,11},{3,1},{4,13},{5,7},{6,15},{7,5},{8,17},{9,0},{1... | collective-permute-start | bytes 786440 | tf_op jit(solution)/shard_map/ppermute | solution.py:337
  3.5 7.5 %collective-permute-start.4 = (bf16[1,4,512,512]{3,2,1,0:T(8,128)(2,1)}, bf16[1,4,512,512]{3,2,1,0:T(8,128)(2,1)S(1)}, u32[]{:S(2)}, u32[]{:S(2)}) collective-permute-start(bf16[1,4,512,512]{3,2,1,0:T(8,128)(2,1)} %left_hbm), channel_id=1, source_target_pairs={{0,1},{1,0},{2,3},{3,2},{4,5},{5,4},{6,7},{7,6},{8,9},{9,8},{10,11... | collective-permute-start | bytes 6291464 | tf_op jit(solution)/shard_map/ppermute | solution.py:339
  3.5 7.5 %collective-permute-start.5 = (bf16[1,4,512,512]{3,2,1,0:T(8,128)(2,1)}, bf16[1,4,512,512]{3,2,1,0:T(8,128)(2,1)S(1)}, u32[]{:S(2)}, u32[]{:S(2)}) collective-permute-start(bf16[1,4,512,512]{3,2,1,0:T(8,128)(2,1)} %right_hbm), channel_id=1, source_target_pairs={{0,1},{1,0},{2,3},{3,2},{4,5},{5,4},{6,7},{7,6},{8,9},{9,8},{10,11... | collective-permute-start | bytes 6291464 | tf_op jit(solution)/shard_map/ppermute | solution.py:339
  5.0 5.9 %collective-permute-start = (bf16[512,256]{1,0:T(8,128)(2,1)S(1)}, bf16[512,256]{1,0:T(8,128)(2,1)S(1)}, u32[]{:S(2)}, u32[]{:S(2)}) collective-permute-start(bf16[512,256]{1,0:T(8,128)(2,1)S(1)} %shard_map.66.own_ref.refs_0_), channel_id=1, source_target_pairs={{0,9},{1,3},{2,11},{3,1},{4,13},{5,7},{6,15},{7,5},{8,17},{9,0},{1... | collective-permute-start | bytes 786440 | tf_op jit(solution)/shard_map/ppermute | solution.py:337
  8.5 2.2 %collective-permute-start.1 = (s32[8,128]{1,0:T(8,128)S(1)}, s32[8,128]{1,0:T(8,128)S(1)}, u32[]{:S(2)}, u32[]{:S(2)}) collective-permute-start(s32[8,128]{1,0:T(8,128)S(1)} %get-tuple-element.34.code_ref.refs_3_), channel_id=1, source_target_pairs={{0,1},{1,0},{2,3},{3,2},{4,5},{5,4},{6,7},{7,6},{8,9},{9,8},{10,11... | collective-permute-start | bytes 12296 | tf_op jit(solution)/shard_map/ppermute | solution.py:341
  9.3 1.7 %collective-permute-start.6 = (bf16[512,256]{1,0:T(8,128)(2,1)S(1)}, bf16[512,256]{1,0:T(8,128)(2,1)S(1)}, u32[]{:S(2)}, u32[]{:S(2)}) collective-permute-start(bf16[512,256]{1,0:T(8,128)(2,1)S(1)} %collective-permute-done.3.refs_1_), channel_id=1, source_target_pairs={{0,1},{1,0},{2,3},{3,2},{4,5},{5,4},{6,7},{7,6},{8,9},{9,8},{10,11... | collective-permute-start | bytes 786440 | tf_op jit(solution)/shard_map/ppermute | solution.py:346
  10.8 1.6 %collective-permute-start.2 = (bf16[512,256]{1,0:T(8,128)(2,1)S(1)}, bf16[512,256]{1,0:T(8,128)(2,1)S(1)}, u32[]{:S(2)}, u32[]{:S(2)}) collective-permute-start(bf16[512,256]{1,0:T(8,128)(2,1)S(1)} %collective-permute-done.refs_1_), channel_id=1, source_target_pairs={{0,1},{1,0},{2,3},{3,2},{4,5},{5,4},{6,7},{7,6},{8,9},{9,8},{10,11... | collective-permute-start | bytes 786440 | tf_op jit(solution)/shard_map/ppermute | solution.py:346
  13.6 5.3 %collective-permute-start.7 = (bf16[1,64,512]{2,1,0:T(8,128)(2,1)S(1)}, bf16[1,64,512]{2,1,0:T(8,128)(2,1)S(1)}, u32[]{:S(2)}, u32[]{:S(2)}) collective-permute-start(bf16[1,64,512]{2,1,0:T(8,128)(2,1)S(1)} %get-tuple-element.40), channel_id=1, source_target_pairs={{0,6},{1,7},{2,4},{3,5},{4,2},{5,3},{6,0},{7,1},{8,14},{9,15},{10,... | collective-permute-start | bytes 196616 | tf_op jit(solution)/shard_map/ppermute | solution.py:361
  16.3 4.1 %collective-permute-start.8 = (bf16[1,64,512]{2,1,0:T(8,128)(2,1)S(1)}, bf16[1,64,512]{2,1,0:T(8,128)(2,1)S(1)}, u32[]{:S(2)}, u32[]{:S(2)}) collective-permute-start(bf16[1,64,512]{2,1,0:T(8,128)(2,1)S(1)} %get-tuple-element.41), channel_id=1, source_target_pairs={{0,3},{1,2},{2,1},{3,0},{4,7},{5,6},{6,5},{7,4},{8,11},{9,10},{10,... | collective-permute-start | bytes 196616 | tf_op jit(solution)/shard_map/ppermute | solution.py:361
  16.5 3.9 %collective-permute-start.9 = (bf16[1,64,512]{2,1,0:T(8,128)(2,1)S(1)}, bf16[1,64,512]{2,1,0:T(8,128)(2,1)S(1)}, u32[]{:S(2)}, u32[]{:S(2)}) collective-permute-start(bf16[1,64,512]{2,1,0:T(8,128)(2,1)S(1)} %get-tuple-element.42), channel_id=1, source_target_pairs={{0,5},{1,4},{2,7},{3,6},{4,1},{5,0},{6,3},{7,2},{8,13},{9,12},{10,... | collective-permute-start | bytes 196616 | tf_op jit(solution)/shard_map/ppermute | solution.py:361
